TPU v7x, 256 devices: a whole 4x4x8 slice. The times are simulated.
256 devices in a mesh: ty: 2 (over core), tx: 4 (over z_lo), pos: 32 (over y, z_hi, x).
Axes of the slice: x: 4, y: 4, z: 8 (z_hi: 2, z_lo: 4; z = z_hi * 4 + z_lo), core: 2. Of those that a mesh axis runs over, the one named last changes fastest.
Arguments:
- object_field: float32 [2, 2, 512, 1024], P(None, None, ('ty', 'pos'), 'tx'), may hold values from -6 to 6
- momentum: float32 [2, 2, 512, 1024], P(None, None, ('ty', 'pos'), 'tx'), may hold values from -12 to 12
- measured: float32 [2, 4, 32, 256, 256], P('ty', 'tx', 'pos'), may hold values from 0 to 2
- illumination: float32 [2, 256, 256], replicated, may hold values from -6 to 6
- slab_phase: float32 [256, 256], replicated, may hold values from -3.140625 to 3.140625
- offsets: int32 [2, 4, 32, 2], P('ty', 'tx'), may hold values from 0 to 128, as said below
- entry_counts: int32 [2, 4], P('ty', 'tx'), may hold values from 8 to 16, as said below
Outputs:
- new_object: float32 [2, 2, 512, 1024], P(None, None, ('ty', 'pos'), 'tx')
- new_momentum: float32 [2, 2, 512, 1024], P(None, None, ('ty', 'pos'), 'tx')
- amplitudes: float32 [2, 4, 32, 256, 256], P('ty', 'tx', 'pos')
Inputs may be any that keep to these rules, and one draw needn't show every extreme that they name: offsets[a, b, k] is the corner of a window of 256 x 256 cells, counted from the corner of tile (a, b) widened by 64 cells on every side. Tile (a, b) uses the first entry_counts[a, b] slots of its list; some tile uses exactly 16 slots in every draw.
All inputs are finite; a program needn't handle non-finite values.
Results may differ from a plain program's by a relative error of at most 0.0003.
Values sent between devices are 32-bit elements; how exact they have to be, the bound alone decides.
A program may use at most 64 MiB of HBM per device.

v0:
```python
import math

import jax
import jax.numpy as jnp
from jax import lax
from jax.sharding import PartitionSpec as P

HIGHEST = lax.Precision.HIGHEST
magnitude_floor = 0.5
momentum_rate = 0.9
step_length = 0.05


def padded(value, sides, width):
    for axis, dim in sides:
        devices, length = (lax.axis_size(axis), value.shape[dim])
        up = [(i, (i + 1) % devices) for i in range(devices - 1)]
        down = [(j, i) for i, j in up]
        last = lax.slice_in_dim(value, length - width, length, axis=dim)
        leading = lax.slice_in_dim(value, 0, width, axis=dim)
        before = lax.ppermute(last, axis, up)
        after = lax.ppermute(leading, axis, down)
        value = jnp.concatenate([before, value, after], axis=dim)
    return value


def copy_for_each(value, axis):
    devices = lax.axis_size(axis)
    return lax.all_to_all(
        jnp.broadcast_to(value[None], (devices, *value.shape)), axis, 0, 0, tiled=True
    )


def joined_along(tiles, dim):
    dims = list(tiles.shape[1:])
    dims[dim] *= tiles.shape[0]
    return jnp.moveaxis(tiles, 0, dim).reshape(dims)


def gather_directly(value, axis, dim):
    tiles = copy_for_each(value, axis)
    return joined_along(tiles, dim)


def cut_along(value, dim, devices):
    before, after = (value.shape[:dim], value.shape[dim + 1 :])
    return jnp.moveaxis(value.reshape(*before, devices, -1, *after), dim, 0)


def sent_and_summed(value, axis, dim):
    devices = lax.axis_size(axis)
    tiles = lax.all_to_all(cut_along(value, dim, devices), axis, 0, 0, tiled=True)
    return jnp.sum(tiles, axis=0)


def tables(length):
    indices = jnp.arange(length, dtype=jnp.int32)
    product = indices[:, None] * indices[None, :] % length
    angles = product.astype(jnp.float32) * (2.0 * math.pi / length)
    factor = 1.0 / math.sqrt(length)
    return (jnp.cos(angles) * factor, jnp.sin(angles) * factor)


def matmul(left, right):
    return jnp.dot(left, right, precision=HIGHEST)


def transform(real_part, imag_part, cosine, sine_table, inverse):
    factor = 1.0 if inverse else -1.0
    right_real = matmul(real_part, cosine) - factor * matmul(imag_part, sine_table)
    right_imag = matmul(imag_part, cosine) + factor * matmul(real_part, sine_table)
    left_real = matmul(cosine, right_real) - factor * matmul(sine_table, right_imag)
    left_imag = matmul(cosine, right_imag) + factor * matmul(sine_table, right_real)
    return (left_real, left_imag)


def complex_product(first_real, first_imag, second_real, second_imag):
    return (
        first_real * second_real - first_imag * second_imag,
        first_real * second_imag + first_imag * second_real,
    )


def forward_window(window, illumination, slab_real, slab_imag, cosine, sine_table):
    entering = complex_product(illumination[0], illumination[1], window[0], window[1])
    spectrum = transform(entering[0], entering[1], cosine, sine_table, False)
    spectrum = complex_product(spectrum[0], spectrum[1], slab_real, slab_imag)
    between = transform(spectrum[0], spectrum[1], cosine, sine_table, True)
    leaving = complex_product(between[0], between[1], window[2], window[3])
    farfield = transform(leaving[0], leaving[1], cosine, sine_table, False)
    return (between, farfield)


def window_gradient(
    window, measured_window, illumination, slab_real, slab_imag, cosine, sine_table
):
    between, farfield = forward_window(
        window, illumination, slab_real, slab_imag, cosine, sine_table
    )
    magnitude = jnp.sqrt(farfield[0] * farfield[0] + farfield[1] * farfield[1])
    keeping = 1.0 - measured_window / jnp.maximum(magnitude, magnitude_floor)
    backward = transform(farfield[0] * keeping, farfield[1] * keeping, cosine, sine_table, True)
    grad_second = complex_product(between[0], -between[1], backward[0], backward[1])
    toward = complex_product(window[2], -window[3], backward[0], backward[1])
    spectrum = transform(toward[0], toward[1], cosine, sine_table, False)
    spectrum = complex_product(spectrum[0], spectrum[1], slab_real, -slab_imag)
    incoming = transform(spectrum[0], spectrum[1], cosine, sine_table, True)
    grad_first = complex_product(illumination[0], -illumination[1], incoming[0], incoming[1])
    return jnp.stack([grad_first[0], grad_first[1], grad_second[0], grad_second[1]])


def fetch(shard, margin):
    shard = padded(shard, (("tx", 2),), margin)
    full_tile = gather_directly(shard, "pos", 1)
    return padded(full_tile, (("ty", 1),), margin)


def fold_edges(received, inner, margin, tile_side, axis_dim):
    widths_low = [(0, 0), (0, 0), (0, 0)]
    widths_high = [(0, 0), (0, 0), (0, 0)]
    widths_low[axis_dim] = (0, tile_side - margin)
    widths_high[axis_dim] = (tile_side - margin, 0)
    lower_piece = lax.slice_in_dim(received, 0, margin, axis=axis_dim)
    upper_piece = lax.slice_in_dim(received, 3 * margin, 4 * margin, axis=axis_dim)
    return inner + jnp.pad(lower_piece, widths_low) + jnp.pad(upper_piece, widths_high)


def shards(object_field, momentum, measured, illumination, slab_phase, offsets, entry_counts):
    width = illumination.shape[-1]
    margin = width // 4
    shard_rows = object_field.shape[2]
    tile_side = object_field.shape[3]
    capacity = measured.shape[2]
    extent = tile_side + 2 * margin
    cosine, sine_table = tables(width)
    slab_real = jnp.cos(slab_phase)
    slab_imag = jnp.sin(slab_phase)
    layers = object_field.reshape(4, shard_rows, tile_side)
    velocity_old = momentum.reshape(4, shard_rows, tile_side)
    places = offsets[0, 0]
    valid_count = entry_counts[0, 0]
    own_measured = measured[0, 0]
    own_index = lax.axis_index("pos")
    zero = jnp.zeros((), jnp.int32)
    last_slot = jnp.clip(valid_count - own_index * capacity, 0, capacity)

    def entry_of(slot_index):
        return own_index * capacity + slot_index

    extended = fetch(layers, margin)

    def accumulate(position, gradient):
        place = places[entry_of(position)]
        corner = (zero, place[0], place[1])
        window = lax.dynamic_slice(extended, corner, (4, width, width))
        term = window_gradient(
            window, own_measured[position], illumination, slab_real, slab_imag, cosine, sine_table
        )
        current = lax.dynamic_slice(gradient, corner, (4, width, width))
        return lax.dynamic_update_slice(gradient, current + term, corner)

    gradient = lax.fori_loop(
        zero, last_slot, accumulate, jnp.zeros((4, extent, extent), jnp.float32)
    )
    column_strips = jnp.concatenate(
        [gradient[:, :, :margin], gradient[:, :, extent - margin :]], axis=2
    )
    column_gains = padded(column_strips, (("tx", 2),), margin)
    inner_columns = fold_edges(
        column_gains, gradient[:, :, margin : margin + tile_side], margin, tile_side, 2
    )
    row_strips = jnp.concatenate(
        [inner_columns[:, :margin], inner_columns[:, extent - margin :]], axis=1
    )
    row_gains = padded(row_strips, (("ty", 1),), margin)
    folded = fold_edges(
        row_gains, inner_columns[:, margin : margin + tile_side], margin, tile_side, 1
    )
    gradient_shard = sent_and_summed(folded, "pos", 1)
    velocity = momentum_rate * velocity_old + gradient_shard
    updated = layers - step_length * velocity
    refreshed = fetch(updated, margin)

    def predict(position, buffer):
        place = places[entry_of(position)]
        window = lax.dynamic_slice(refreshed, (zero, place[0], place[1]), (4, width, width))
        farfield = forward_window(window, illumination, slab_real, slab_imag, cosine, sine_table)[1]
        magnitude = jnp.sqrt(farfield[0] * farfield[0] + farfield[1] * farfield[1])
        return magnitude[None]

    buffer = lax.fori_loop(
        zero, last_slot, predict, jnp.zeros((own_measured.shape[0], width, width), jnp.float32)
    )
    return (
        updated.reshape(2, 2, shard_rows, tile_side),
        velocity.reshape(2, 2, shard_rows, tile_side),
        buffer[None, None],
    )


def solution(mesh):
    placed = (
        P(None, None, ("ty", "pos"), "tx"),
        P(None, None, ("ty", "pos"), "tx"),
        P("ty", "tx", "pos", None, None),
        P(),
        P(),
        P("ty", "tx", None, None),
        P("ty", "tx"),
    )
    return jax.shard_map(
        shards,
        mesh=mesh,
        in_specs=placed,
        out_specs=(
            P(None, None, ("ty", "pos"), "tx"),
            P(None, None, ("ty", "pos"), "tx"),
            P("ty", "tx", "pos", None, None),
        ),
        check_vma=False,
    )
```

profile of v0, /device:TPU:1, one launch (start us, length us, event | category | flops | bytes accessed | tf_op | source)
XLA Modules:
  0.0 354.2 jit_solution(15845564695651137097)
XLA Ops:
  1.4 4.4 %collective-permute-start = (f32[4,8,64]{2,1,0:T(8,128)S(1)}, f32[4,8,64]{2,1,0:T(8,128)S(1)}, u32[]{:S(2)}, u32[]{:S(2)}) collective-permute-start(f32[4,8,64]{2,1,0:T(8,128)S(1)} %get-tuple-element.722), channel_id=1, source_target_pairs={{0,32},{32,64},{64,96},{1,33},{33,65},{65,97},{2,34},{34,66},{66,9... | collective-permute-start | bytes 24584 | tf_op jit(solution)/shard_map/ppermute | solution.py:21
  7.1 3.4 collective-permute-done.1
  12.7 12.7 %all-to-all-start = ((f32[32,4,8,384]{3,2,1,0:T(8,128)}), f32[32,4,8,384]{3,2,1,0:T(8,128)}, u32[]{:S(2)}, u32[]{:S(2)}) async-start(f32[32,4,8,384]{3,2,1,0:T(8,128)} %broadcast_in_dim.14), calls=%async_computation | async-start | bytes 3145728 | tf_op jit(solution)/shard_map/all_to_all | solution.py:29
  25.5 27.2 %all-to-all-done = f32[32,4,8,384]{3,2,1,0:T(8,128)} async-done(((f32[32,4,8,384]{3,2,1,0:T(8,128)}), f32[32,4,8,384]{3,2,1,0:T(8,128)}, u32[]{:S(2)}, u32[]{:S(2)}) %all-to-all-start) | async-done | bytes 1572896 | tf_op jit(solution)/shard_map/all_to_all | solution.py:29
  52.7 1.5 copy.59
  56.5 18.3 %collective-permute-start.3 = (f32[4,64,384]{2,1,0:T(8,128)}, f32[4,64,384]{2,1,0:T(8,128)}, u32[]{:S(2)}, u32[]{:S(2)}) collective-permute-start(f32[4,64,384]{2,1,0:T(8,128)} %get-tuple-element.716), channel_id=1, source_target_pairs={{128,0},{129,1},{130,2},{131,3},{132,4},{133,5},{134,6},{135,7},{1... | collective-permute-start | bytes 1179656 | tf_op jit(solution)/shard_map/ppermute | solution.py:22
  78.6 2.6 pad_maximum_fusion
  81.2 1.6 broadcast_in_dim.12
  82.7 97.7 %while.25 = (s32[]{:T(128)}, f32[4,384,384]{1,2,0:T(8,128)}, s32[]{:T(128)}, s32[]{:T(128)}, s32[32,2]{0,1:T(2,128)S(1)}, /*index=5*/f32[2,256,256]{1,2,0:T(8,12...) while((s32[]{:T(128)}, f32[4,384,384]{1,2,0:T(8,128)}, ...), condition=%wide.region_1.2_spmd.clone.clone, body=%wide.region_0.1_spmd.clone.clone.sunk | while | flops 9717678080 | bytes 49807748 | solution.py:162
  87.5 1.7 fusion.750
  91.1 1.5 fusion.756
  94.1 1.5 fusion.753
  97.0 1.5 fusion.757
  100.0 2.1 multiply_subtract_fusion.8
  103.6 1.5 convolution_subtract_fusion.12
  109.5 1.5 fusion.762
  112.7 1.7 fusion.764
  115.9 1.5 fusion.769
  118.9 1.5 fusion.766
  121.8 1.5 fusion.770
  124.8 1.8 fusion.772
  133.9 1.5 fusion.776
  136.9 2.0 fusion.778
  146.3 1.5 fusion.784
  147.7 1.6 fusion.785
  149.4 1.5 multiply_subtract_fusion.9
  152.4 1.5 convolution_subtract_fusion.14
  155.4 1.5 convolution_add_fusion.14
  158.3 1.5 fusion.789
  159.8 1.7 fusion.790
  161.5 1.5 fusion.791
  163.0 1.8 maximum_add_fusion.2
  164.8 11.0 %dynamic_update_slice.7 = f32[4,384,384]{1,2,0:T(8,128)} dynamic-update-slice(f32[4,384,384]{1,2,0:T(8,128)} %get-tuple-element.942, f32[4,256,256]{1,2,0:T(8,128)S(1)} %maximum_add_fusion.2, s32[]{:T(128)} %constant.58.clone.1..sunk, s32[]{:T(128)S(6)} %select_n.437, s32[]{:T(128)S(6)} %select_n.438) | dynamic-update-slice | bytes 2097156 | tf_op jit(solution)/shard_map/while/body/dynamic_update_slice | solution.py:160
  180.4 2.1 fusion.488
  182.5 5.2 %collective-permute-start.4 = (f32[4,384,64]{1,2,0:T(8,128)}, f32[4,384,64]{1,2,0:T(8,128)}, u32[]{:S(2)}, u32[]{:S(2)}) collective-permute-start(f32[4,384,64]{1,2,0:T(8,128)} %get-tuple-element.709), channel_id=1, source_target_pairs={{0,32},{32,64},{64,96},{1,33},{33,65},{65,97},{2,34},{34,66},{66,9... | collective-permute-start | bytes 1179656 | tf_op jit(solution)/shard_map/ppermute | solution.py:21
  189.0 2.0 copy.38
  191.1 3.8 %collective-permute-done.4 = f32[4,384,64]{1,2,0:T(8,128)} collective-permute-done((f32[4,384,64]{1,2,0:T(8,128)}, f32[4,384,64]{1,2,0:T(8,128)}, u32[]{:S(2)}, u32[]{:S(2)}) %collective-permute-start.4) | collective-permute-done | bytes 393248 | tf_op jit(solution)/shard_map/ppermute | solution.py:21
  194.8 2.2 copy.39
  197.0 2.7 collective-permute-done.5
  199.7 2.2 copy.40
  201.8 2.0 fusion.476
  205.2 3.1 collective-permute-start.7
  209.7 32.7 %all_to_all.15 = f32[32,4,8,256]{3,2,1,0:T(8,128)S(1)} all-to-all(f32[32,4,8,256]{3,2,1,0:T(8,128)S(1)} %copy.41), channel_id=1, replica_groups=mesh['ty'=2,'tx'=4,'pos'=32] {'pos'}, dimensions={0} | all-to-all | bytes 2097152 | tf_op jit(solution)/shard_map/all_to_all | solution.py:52
  243.1 4.1 %collective-permute-start.8 = (f32[4,8,64]{2,1,0:T(8,128)S(1)}, f32[4,8,64]{2,1,0:T(8,128)S(1)}, u32[]{:S(2)}, u32[]{:S(2)}) collective-permute-start(f32[4,8,64]{2,1,0:T(8,128)S(1)} %get-tuple-element.719), channel_id=1, source_target_pairs={{0,32},{32,64},{64,96},{1,33},{33,65},{65,97},{2,34},{34,66},{66,9... | collective-permute-start | bytes 24584 | tf_op jit(solution)/shard_map/ppermute | solution.py:21
  248.5 3.2 collective-permute-done.9
  252.0 32.2 %all_to_all.16 = f32[32,4,8,384]{3,2,1,0:T(8,128)S(1)} all-to-all(f32[32,4,8,384]{3,2,1,0:T(8,128)S(1)} %broadcast_in_dim.29), channel_id=1, replica_groups=mesh['ty'=2,'tx'=4,'pos'=32] {'pos'}, dimensions={0} | all-to-all | bytes 3145728 | tf_op jit(solution)/shard_map/all_to_all | solution.py:29
  286.5 16.0 %collective-permute-start.11 = (f32[4,64,384]{2,1,0:T(8,128)}, f32[4,64,384]{2,1,0:T(8,128)S(1)}, u32[]{:S(2)}, u32[]{:S(2)}) collective-permute-start(f32[4,64,384]{2,1,0:T(8,128)} %get-tuple-element.712), channel_id=1, source_target_pairs={{128,0},{129,1},{130,2},{131,3},{132,4},{133,5},{134,6},{135,7},{1... | collective-permute-start | bytes 1179656 | tf_op jit(solution)/shard_map/ppermute | solution.py:22
  302.5 1.5 collective-permute-done.11
  304.0 1.6 pad_maximum_fusion.1
  306.3 45.9 %while.26 = (s32[]{:T(128)}, f32[1,256,256]{1,2,0:T(8,128)}, s32[]{:T(128)}, f32[2,256,256]{1,2,0:T(8,128)S(1)}, s32[]{:T(128)}, /*index=5*/s32[32,2]{0,1:T(2,12...) while((s32[]{:T(128)}, f32[1,256,256]{1,2,0:T(8,128)}, ...), condition=%wide.region_4.5_spmd.clone.clone, body=%wide.region_3.4_spmd.clone.clone.sunk | while | flops 4858118144 | bytes 23855460 | solution.py:191
  310.9 1.7 fusion.817
  314.5 1.5 fusion.822
  317.4 1.5 fusion.819
  320.4 1.5 fusion.823
  323.4 1.9 multiply_add_fusion.5
  326.8 1.5 convolution_add_fusion.15
  329.7 1.5 convolution_subtract_fusion.15
  332.7 1.5 fusion.828
  335.9 1.7 fusion.830
  339.1 1.5 fusion.835
  342.1 1.5 fusion.832
  345.0 1.5 fusion.836
  348.0 2.2 fusion.838
  352.2 1.8 copy.45
  (100 shorter events, 78.8 us)
Async XLA Ops:
  1.4 5.7 %collective-permute-start = (f32[4,8,64]{2,1,0:T(8,128)S(1)}, f32[4,8,64]{2,1,0:T(8,128)S(1)}, u32[]{:S(2)}, u32[]{:S(2)}) collective-permute-start(f32[4,8,64]{2,1,0:T(8,128)S(1)} %get-tuple-element.722), channel_id=1, source_target_pairs={{0,32},{32,64},{64,96},{1,33},{33,65},{65,97},{2,34},{34,66},{66,9... | collective-permute-start | bytes 24584 | tf_op jit(solution)/shard_map/ppermute | solution.py:21
  5.8 4.7 %collective-permute-start.1 = (f32[4,8,64]{2,1,0:T(8,128)S(1)}, f32[4,8,64]{2,1,0:T(8,128)S(1)}, u32[]{:S(2)}, u32[]{:S(2)}) collective-permute-start(f32[4,8,64]{2,1,0:T(8,128)S(1)} %get-tuple-element.723), channel_id=1, source_target_pairs={{32,0},{64,32},{96,64},{33,1},{65,33},{97,65},{34,2},{66,34},{98,6... | collective-permute-start | bytes 24584 | tf_op jit(solution)/shard_map/ppermute | solution.py:22
  11.3 14.1 %copy-start.1 = (f32[256,256]{1,0:T(8,128)S(1)}, f32[256,256]{1,0:T(8,128)}, u32[]{:S(2)}) copy-start(f32[256,256]{1,0:T(8,128)} %param.15) | copy-start | bytes 786436
  12.7 40.1 %all-to-all-start = ((f32[32,4,8,384]{3,2,1,0:T(8,128)}), f32[32,4,8,384]{3,2,1,0:T(8,128)}, u32[]{:S(2)}, u32[]{:S(2)}) async-start(f32[32,4,8,384]{3,2,1,0:T(8,128)} %broadcast_in_dim.14), calls=%async_computation | async-start | bytes 3145728 | tf_op jit(solution)/shard_map/all_to_all | solution.py:29
  54.3 23.4 %copy-start.2 = (f32[1,1,1,256,256]{4,3,2,1,0:T(8,128)S(1)}, f32[1,1,1,256,256]{4,3,2,1,0:T(8,128)}, u32[]{:S(2)}) copy-start(f32[1,1,1,256,256]{4,3,2,1,0:T(8,128)} %param.13) | copy-start | bytes 786436
  55.2 23.3 %collective-permute-start.2 = (f32[4,64,384]{2,1,0:T(8,128)}, f32[4,64,384]{2,1,0:T(8,128)S(1)}, u32[]{:S(2)}, u32[]{:S(2)}) collective-permute-start(f32[4,64,384]{2,1,0:T(8,128)} %get-tuple-element.715), channel_id=1, source_target_pairs={{0,128},{1,129},{2,130},{3,131},{4,132},{5,133},{6,134},{7,135},{8... | collective-permute-start | bytes 1179656 | tf_op jit(solution)/shard_map/ppermute | solution.py:21
  56.5 22.0 %collective-permute-start.3 = (f32[4,64,384]{2,1,0:T(8,128)}, f32[4,64,384]{2,1,0:T(8,128)}, u32[]{:S(2)}, u32[]{:S(2)}) collective-permute-start(f32[4,64,384]{2,1,0:T(8,128)} %get-tuple-element.716), channel_id=1, source_target_pairs={{128,0},{129,1},{130,2},{131,3},{132,4},{133,5},{134,6},{135,7},{1... | collective-permute-start | bytes 1179656 | tf_op jit(solution)/shard_map/ppermute | solution.py:22
  81.2 1.6 copy-start.3
  81.2 1.6 copy-start.4
  182.5 12.3 %collective-permute-start.4 = (f32[4,384,64]{1,2,0:T(8,128)}, f32[4,384,64]{1,2,0:T(8,128)}, u32[]{:S(2)}, u32[]{:S(2)}) collective-permute-start(f32[4,384,64]{1,2,0:T(8,128)} %get-tuple-element.709), channel_id=1, source_target_pairs={{0,32},{32,64},{64,96},{1,33},{33,65},{65,97},{2,34},{34,66},{66,9... | collective-permute-start | bytes 1179656 | tf_op jit(solution)/shard_map/ppermute | solution.py:21
  187.7 11.9 %collective-permute-start.5 = (f32[4,384,64]{1,2,0:T(8,128)}, f32[4,384,64]{1,2,0:T(8,128)}, u32[]{:S(2)}, u32[]{:S(2)}) collective-permute-start(f32[4,384,64]{1,2,0:T(8,128)} %get-tuple-element.710), channel_id=1, source_target_pairs={{32,0},{64,32},{96,64},{33,1},{65,33},{97,65},{34,2},{66,34},{98,6... | collective-permute-start | bytes 1179656 | tf_op jit(solution)/shard_map/ppermute | solution.py:22
  203.9 4.4 %collective-permute-start.6 = (f32[4,64,256]{2,1,0:T(8,128)S(1)}, f32[4,64,256]{2,1,0:T(8,128)S(1)}, u32[]{:S(2)}, u32[]{:S(2)}) collective-permute-start(f32[4,64,256]{2,1,0:T(8,128)S(1)} %get-tuple-element.713), channel_id=1, source_target_pairs={{0,128},{1,129},{2,130},{3,131},{4,132},{5,133},{6,134},{7,135},{8... | collective-permute-start | bytes 786440 | tf_op jit(solution)/shard_map/ppermute | solution.py:21
  205.2 4.2 %collective-permute-start.7 = (f32[4,64,256]{2,1,0:T(8,128)S(1)}, f32[4,64,256]{2,1,0:T(8,128)S(1)}, u32[]{:S(2)}, u32[]{:S(2)}) collective-permute-start(f32[4,64,256]{2,1,0:T(8,128)S(1)} %get-tuple-element.714), channel_id=1, source_target_pairs={{128,0},{129,1},{130,2},{131,3},{132,4},{133,5},{134,6},{135,7},{1... | collective-permute-start | bytes 786440 | tf_op jit(solution)/shard_map/ppermute | solution.py:22
  209.5 32.9 %copy-start = (f32[2,2,8,256]{3,2,1,0:T(8,128)S(1)}, f32[2,2,8,256]{3,2,1,0:T(8,128)}, u32[]{:S(2)}) copy-start(f32[2,2,8,256]{3,2,1,0:T(8,128)} %param.11) | copy-start | bytes 98308
  209.5 32.9 %copy-start.5 = (f32[2,2,8,256]{3,2,1,0:T(8,128)S(1)}, f32[2,2,8,256]{3,2,1,0:T(8,128)}, u32[]{:S(2)}) copy-start(f32[2,2,8,256]{3,2,1,0:T(8,128)} %param.12) | copy-start | bytes 98308
  243.1 5.4 %collective-permute-start.8 = (f32[4,8,64]{2,1,0:T(8,128)S(1)}, f32[4,8,64]{2,1,0:T(8,128)S(1)}, u32[]{:S(2)}, u32[]{:S(2)}) collective-permute-start(f32[4,8,64]{2,1,0:T(8,128)S(1)} %get-tuple-element.719), channel_id=1, source_target_pairs={{0,32},{32,64},{64,96},{1,33},{33,65},{65,97},{2,34},{34,66},{66,9... | collective-permute-start | bytes 24584 | tf_op jit(solution)/shard_map/ppermute | solution.py:21
  247.2 4.5 %collective-permute-start.9 = (f32[4,8,64]{2,1,0:T(8,128)S(1)}, f32[4,8,64]{2,1,0:T(8,128)S(1)}, u32[]{:S(2)}, u32[]{:S(2)}) collective-permute-start(f32[4,8,64]{2,1,0:T(8,128)S(1)} %get-tuple-element.720), channel_id=1, source_target_pairs={{32,0},{64,32},{96,64},{33,1},{65,33},{97,65},{34,2},{66,34},{98,6... | collective-permute-start | bytes 24584 | tf_op jit(solution)/shard_map/ppermute | solution.py:22
  285.2 17.3 %collective-permute-start.10 = (f32[4,64,384]{2,1,0:T(8,128)}, f32[4,64,384]{2,1,0:T(8,128)S(1)}, u32[]{:S(2)}, u32[]{:S(2)}) collective-permute-start(f32[4,64,384]{2,1,0:T(8,128)} %get-tuple-element.711), channel_id=1, source_target_pairs={{0,128},{1,129},{2,130},{3,131},{4,132},{5,133},{6,134},{7,135},{8... | collective-permute-start | bytes 1179656 | tf_op jit(solution)/shard_map/ppermute | solution.py:21
  286.5 17.5 %collective-permute-start.11 = (f32[4,64,384]{2,1,0:T(8,128)}, f32[4,64,384]{2,1,0:T(8,128)S(1)}, u32[]{:S(2)}, u32[]{:S(2)}) collective-permute-start(f32[4,64,384]{2,1,0:T(8,128)} %get-tuple-element.712), channel_id=1, source_target_pairs={{128,0},{129,1},{130,2},{131,3},{132,4},{133,5},{134,6},{135,7},{1... | collective-permute-start | bytes 1179656 | tf_op jit(solution)/shard_map/ppermute | solution.py:22
where the time goes:
time: 358 us; the launch traced here: 354 us
  matrix products  110 us (31%)
  starting transfers between devices  71.4 us (20%)
  blocking collectives  64.8 us (18%)
  waiting for transfers between devices  42.8 us (12%)
  local copies, waits for them, and re-layouts  38.6 us (11%)
  loops' own time  15.3 us (4%)
  other arithmetic  9.94 us (3%)
    dot_general x72, matrix products, matmul(): return jnp.dot(left, right, precision=HIGHEST)  110 us
    ppermute x6, starting transfers between devices, padded(): after = lax.ppermute(leading, axis, down)  41.2 us
    all_to_all x1, blocking collectives, sent_and_summed(): lax.all_to_all(cut_along(value, dim, devices), axis, 0, 0, tiled=True)  32.7 us
    all_to_all x1, blocking collectives, copy_for_each(): lax.all_to_all(jnp.broadcast_to(value[None], (devices, *value.shape)), ax...  32.2 us
    all_to_all x1, waiting for transfers between devices, copy_for_each(): lax.all_to_all(jnp.broadcast_to(value[None], (devices, *value.shape)), ax...  27.2 us
    ppermute x6, starting transfers between devices, padded(): before = lax.ppermute(last, axis, up)  17.5 us
    all_to_all x1, starting transfers between devices, copy_for_each(): lax.all_to_all(jnp.broadcast_to(value[None], (devices, *value.shape)), ax...  12.7 us
    ppermute x6, waiting for transfers between devices, padded(): after = lax.ppermute(leading, axis, down)  11.8 us
  transfers between devices with their start and end apart: 13, of which 7 were waited for; matrix products, arithmetic and copies ran while one was open for 2% of the time, Pallas kernels for 0%

commit v1 on v0

v1 whole, which is shorter than its diff:
```python
import functools
import math

import jax
import jax.numpy as jnp
import numpy as np
from jax import lax
from jax.experimental import pallas as pl
from jax.experimental.pallas import tpu as pltpu
from jax.sharding import PartitionSpec as P

f32 = jnp.float32
bf16 = jnp.bfloat16
MESH = pl.DeviceIdType.MESH
magnitude_floor = 0.5
momentum_rate = 0.9
step_length = 0.05
W = 256
MARGIN = 64
ROLES = [(s, h, k) for s in range(2) for h in range(2) for k in range(3)]
VMEM_LIMIT = 48 * 1024 * 1024


def tables(length):
    indices = np.arange(length)
    angles = (indices[:, None] * indices[None, :] % length) * (2.0 * math.pi / length)
    c = np.cos(angles) / math.sqrt(length)
    s = np.sin(angles) / math.sqrt(length)

    def halves(value):
        value = value.astype(np.float32)
        high = value.astype(jnp.bfloat16)
        low = (value - high.astype(np.float32)).astype(jnp.bfloat16)
        return np.stack([high, low])

    right = halves(np.concatenate([c, s], axis=0))
    forward = halves(np.block([[c, s], [-s, c]]))
    inverse = halves(np.block([[c, -s], [s, c]]))
    return right, np.stack([forward, inverse])


def coordinates():
    ty = lax.axis_index("ty")
    tx = lax.axis_index("tx")
    pos = lax.axis_index("pos")
    return ty, tx, pos, pos // 8, (pos // 4) % 2, pos % 4


def peer(ty, tx, pos):
    return {"ty": ty, "tx": tx, "pos": pos}


def position(y, zh, x):
    return y * 8 + zh * 4 + x


def close_peer(role, outward):
    s, h, k = role
    ty, tx, pos, y, zh, x = coordinates()
    step = (0, 3, 1)[k] if outward else (0, 1, 3)[k]
    other_ty = 1 - ty if s else ty
    other_zh = 1 - zh if h else zh
    return other_ty, (tx + step) % 4, other_zh, position(y, other_zh, x)


def enter(both_ways):
    ty, tx, pos, y, zh, x = coordinates()
    barrier = pltpu.get_barrier_semaphore()
    for role in ROLES:
        if role != (0, 0, 0):
            other_ty, other_tx, _, other_pos = close_peer(role, True)
            pl.semaphore_signal(barrier, inc=1, device_id=peer(other_ty, other_tx, other_pos), device_id_type=MESH)
    me = y * 4 + x
    small = (y % 2) * 4 + x

    def greet(start, count, modulus):
        def body(j, carry):
            t = (start + j) % modulus
            pl.semaphore_signal(
                barrier, inc=1, device_id=peer(ty, tx, position(t // 4, zh, t % 4)), device_id_type=MESH
            )
            return carry

        lax.fori_loop(0, count, body, 0)

    @pl.when(y < 2)
    def _():
        greet(me + 1, 15, 16)
        pl.semaphore_wait(barrier, 11 + (15 if both_ways else 7))

    @pl.when(y >= 2)
    def _():
        if both_ways:
            greet(small, 8, 8)
        pl.semaphore_wait(barrier, 11 + 8)


def gather_close(src, held, send_sem, recv_sem):
    ty, tx, pos, y, zh, x = coordinates()
    copies = []
    for index, role in enumerate(ROLES):
        if role == (0, 0, 0):
            continue
        k = role[2]
        other_ty, other_tx, _, other_pos = close_peer(role, True)
        if k == 0:
            source, target = src, held.at[ty, 0, :, zh]
        else:
            lanes = pl.ds(128 * (k - 1), 128)
            source, target = src.at[:, :, lanes], held.at[ty, 1, :, zh, :, lanes]
        copy = pltpu.make_async_remote_copy(
            src_ref=source,
            dst_ref=target,
            send_sem=send_sem.at[index],
            recv_sem=recv_sem.at[index],
            device_id=peer(other_ty, other_tx, other_pos),
            device_id_type=MESH,
        )
        copy.start()
        copies.append(copy)
    held[ty, 0, :, zh] = src[...]
    return copies


def row_swap(row_start):
    ty, tx, pos, y, zh, x = coordinates()
    shape = (2, 8, 256)
    row = (
        y * 64
        + x * 8
        + lax.broadcasted_iota(jnp.int32, shape, 0) * 32
        + lax.broadcasted_iota(jnp.int32, shape, 1)
    )
    return ((row < MARGIN) & (row_start > row + MARGIN)) | ((row >= 192) & (row > row_start + 191))


def column_swap(column_start):
    column = lax.broadcasted_iota(jnp.int32, (2, 8, 256), 2)
    return ((column < MARGIN) & (column_start > column + MARGIN)) | (
        (column >= 192) & (column > column_start + 191)
    )


def edge_columns():
    tx = lax.axis_index("tx")
    column = lax.broadcasted_iota(jnp.int32, (2, 8, 256), 2)
    missing = ((column < 128) & (tx == 3)) | ((column >= 128) & (tx == 0))
    return jnp.where(missing, 0.0, 1.0)


def edge_rows():
    ty, tx, pos, y, zh, x = coordinates()
    present = ((ty == 0) & (y == 0)) | ((ty == 1) & (y == 3))
    return jnp.where(present, 1.0, 0.0)


def gather_far(offsets, held, blocks, window, send_sem, recv_sem):
    ty, tx, pos, y, zh, x = coordinates()
    base = (y % 2) * 4 + x
    me = y * 4 + x
    columns_real = edge_columns()
    rows_real = edge_rows()

    def target_of(j):
        t = (base + j) % 8
        return position(t // 4, zh, t % 4)

    def copy_to(j):
        return pltpu.make_async_remote_copy(
            src_ref=blocks.at[j],
            dst_ref=window.at[:, pl.ds(2 * y, 2), x],
            send_sem=send_sem.at[j],
            recv_sem=recv_sem.at[me],
            device_id=peer(ty, tx, target_of(j)),
            device_id_type=MESH,
        )

    for j in range(8):
        target = target_of(j)
        swap_rows = row_swap(offsets[target, 0])
        swap_columns = column_swap(offsets[target, 1])
        for layer in range(4):
            own = jnp.where(swap_columns, held[ty, 1, layer] * columns_real, held[ty, 0, layer])
            sibling = jnp.where(swap_columns, held[1 - ty, 1, layer] * columns_real, held[1 - ty, 0, layer])
            blocks[j, layer] = jnp.where(swap_rows, sibling * rows_real, own)
        if j == 0:

            @pl.when(y >= 2)
            def _():
                copy_to(0).start()

            @pl.when(y < 2)
            def _():
                window[:, pl.ds(2 * y, 2), x] = blocks[0]

        else:
            copy_to(j).start()

    @pl.when(y < 2)
    def _():
        def arrive(j, carry):
            s = (me + j) % 16
            pltpu.make_async_remote_copy(
                src_ref=blocks.at[0],
                dst_ref=window.at[:, pl.ds(2 * (s // 4), 2), s % 4],
                send_sem=send_sem.at[0],
                recv_sem=recv_sem.at[s],
                device_id=peer(ty, tx, position(s // 4, zh, s % 4)),
                device_id_type=MESH,
            ).wait_recv()
            return carry

        lax.fori_loop(1, 16, arrive, 0)

    @pl.when(y >= 2)
    def _():
        copy_to(0).wait_send()

    for j in range(1, 8):
        copy_to(j).wait_send()


def gather_kernel(offsets, rows, window, held, blocks, send_close, recv_close, send_far, recv_far):
    enter(False)
    for copy in gather_close(rows, held, send_close, recv_close):
        copy.wait()
    gather_far(offsets, held, blocks, window, send_far, recv_far)


def return_kernel(
    offsets,
    rows,
    momentum,
    gradient,
    new_rows,
    new_momentum,
    window,
    arrived,
    sums,
    parts_own,
    parts_side,
    held,
    blocks,
    send_return,
    recv_return,
    send_sum,
    recv_sum,
    send_close,
    recv_close,
    send_far,
    recv_far,
):
    ty, tx, pos, y, zh, x = coordinates()
    enter(True)
    me = y * 4 + x
    base = (y % 2) * 4 + x

    def copy_to(j):
        t = (me + j) % 16
        return pltpu.make_async_remote_copy(
            src_ref=gradient.at[:, pl.ds(2 * (t // 4), 2), t % 4],
            dst_ref=arrived.at[base],
            send_sem=send_return.at[j],
            recv_sem=recv_return.at[base],
            device_id=peer(ty, tx, position(t // 4, zh, t % 4)),
            device_id_type=MESH,
        )

    def copy_from(s):
        return pltpu.make_async_remote_copy(
            src_ref=gradient.at[:, pl.ds(0, 2), 0],
            dst_ref=arrived.at[s],
            send_sem=send_return.at[0],
            recv_sem=recv_return.at[s],
            device_id=peer(ty, tx, position(s // 4, zh, s % 4)),
            device_id_type=MESH,
        )

    @pl.when(y < 2)
    def _():
        def leave(j, carry):
            copy_to(j).start()
            return carry

        lax.fori_loop(1, 16, leave, 0)
        arrived[base] = gradient[:, pl.ds(2 * y, 2), x]

    @pl.when(y >= 2)
    def _():
        copy_from(base).wait_recv()

    for j in range(1, 8):
        copy_from((base + j) % 8).wait_recv()

    columns_real = edge_columns()
    rows_real = edge_rows()
    swaps = []
    for j in range(8):
        target = position(j // 4, zh, j % 4)
        swaps.append((row_swap(offsets[target, 0]), column_swap(offsets[target, 1])))
    for layer in range(4):
        own = jnp.zeros((2, 8, 256), f32)
        own_side, sibling, sibling_side = own, own, own
        for j in range(8):
            swap_rows, swap_columns = swaps[j]
            block = arrived[j, layer]
            mine = jnp.where(swap_rows, 0.0, block)
            theirs = jnp.where(swap_rows, block, 0.0)
            own = own + jnp.where(swap_columns, 0.0, mine)
            own_side = own_side + jnp.where(swap_columns, mine, 0.0)
            sibling = sibling + jnp.where(swap_columns, 0.0, theirs)
            sibling_side = sibling_side + jnp.where(swap_columns, theirs, 0.0)
        sums[ty, 0, layer] = own
        sums[ty, 1, layer] = own_side * columns_real
        sums[1 - ty, 0, layer] = sibling * rows_real
        sums[1 - ty, 1, layer] = sibling_side * columns_real * rows_real

    copies = []
    for index, role in enumerate(ROLES):
        if role == (0, 0, 0):
            continue
        s, h, k = role
        other_ty, other_tx, other_zh, other_pos = close_peer(role, False)
        if k == 0:
            source, target = sums.at[other_ty, 0, :, other_zh], parts_own.at[2 * s + h]
        else:
            lanes = pl.ds(128 * (k - 1), 128)
            source = sums.at[other_ty, 1, :, other_zh, :, lanes]
            target = parts_side.at[2 * s + h, :, :, lanes]
        copy = pltpu.make_async_remote_copy(
            src_ref=source,
            dst_ref=target,
            send_sem=send_sum.at[index],
            recv_sem=recv_sum.at[index],
            device_id=peer(other_ty, other_tx, other_pos),
            device_id_type=MESH,
        )
        copy.start()
        copies.append(copy)
    for copy in copies:
        copy.wait()
    total = sums[ty, 0, :, zh]
    for part in range(4):
        if part:
            total = total + parts_own[part]
        total = total + parts_side[part]
    velocity = momentum_rate * momentum[...] + total
    new_momentum[...] = velocity
    new_rows[...] = rows[...] - step_length * velocity
    for copy in gather_close(new_rows, held, send_close, recv_close):
        copy.wait()
    gather_far(offsets, held, blocks, window, send_far, recv_far)

    @pl.when(y < 2)
    def _():
        def left(j, carry):
            copy_to(j).wait_send()
            return carry

        lax.fori_loop(1, 16, left, 0)


def split(value):
    high = value.astype(bf16)
    return high, (value - high.astype(f32)).astype(bf16)


def product(left, right):
    return jnp.dot(left, right, preferred_element_type=f32)


def transform(real_part, imag_part, right, left, inverse):
    def stacked(r, i):
        if inverse:
            return jnp.concatenate([jnp.concatenate([r, -i], 1), jnp.concatenate([i, r], 1)], 0)
        return jnp.concatenate([jnp.concatenate([r, i], 1), jnp.concatenate([i, -r], 1)], 0)

    real_high, real_low = split(real_part)
    imag_high, imag_low = split(imag_part)
    high = stacked(real_high, imag_high)
    low = stacked(real_low, imag_low)
    middle = product(high, right[0]) + product(low, right[0]) + product(high, right[1])
    high, low = split(middle)
    which = 1 if inverse else 0
    result = product(left[which, 0], high) + product(left[which, 0], low) + product(left[which, 1], high)
    return result[:W], result[W:]


def complex_product(first_real, first_imag, second_real, second_imag):
    return (
        first_real * second_real - first_imag * second_imag,
        first_real * second_imag + first_imag * second_real,
    )


def shifted_probe(offsets, illumination):
    pos = lax.axis_index("pos")
    down = (offsets[pos, 0] + 192) % 256
    across = (offsets[pos, 1] + 192) % 256
    return [pltpu.roll(pltpu.roll(illumination[part], down, 0), across, 1) for part in range(2)]


def forward(window, probe, slab, right, left):
    entering = complex_product(probe[0], probe[1], window[0], window[1])
    spectrum = transform(entering[0], entering[1], right, left, False)
    spectrum = complex_product(spectrum[0], spectrum[1], slab[0], slab[1])
    between = transform(spectrum[0], spectrum[1], right, left, True)
    leaving = complex_product(between[0], between[1], window[2], window[3])
    return between, transform(leaving[0], leaving[1], right, left, False)


def gradient_kernel(offsets, counts, window, measured, illumination, slab, right, left, gradient):
    pos = lax.axis_index("pos")
    live = pos < counts[0, 0]

    @pl.when(jnp.logical_not(live))
    def _():
        gradient[...] = jnp.zeros_like(gradient)

    @pl.when(live)
    def _():
        probe = shifted_probe(offsets, illumination)
        between, farfield = forward(window, probe, slab, right, left)
        magnitude = jnp.sqrt(farfield[0] * farfield[0] + farfield[1] * farfield[1])
        keeping = 1.0 - measured[...] / jnp.maximum(magnitude, magnitude_floor)
        backward = transform(farfield[0] * keeping, farfield[1] * keeping, right, left, True)
        grad_second = complex_product(between[0], -between[1], backward[0], backward[1])
        gradient[2] = grad_second[0]
        gradient[3] = grad_second[1]
        toward = complex_product(window[2], -window[3], backward[0], backward[1])
        spectrum = transform(toward[0], toward[1], right, left, False)
        spectrum = complex_product(spectrum[0], spectrum[1], slab[0], -slab[1])
        incoming = transform(spectrum[0], spectrum[1], right, left, True)
        grad_first = complex_product(probe[0], -probe[1], incoming[0], incoming[1])
        gradient[0] = grad_first[0]
        gradient[1] = grad_first[1]


def predict_kernel(offsets, counts, window, illumination, slab, right, left, amplitude):
    pos = lax.axis_index("pos")
    live = pos < counts[0, 0]

    @pl.when(jnp.logical_not(live))
    def _():
        amplitude[...] = jnp.zeros_like(amplitude)

    @pl.when(live)
    def _():
        probe = shifted_probe(offsets, illumination)
        farfield = forward(window, probe, slab, right, left)[1]
        amplitude[...] = jnp.sqrt(farfield[0] * farfield[0] + farfield[1] * farfield[1])


def specs(count, scalars):
    return [pl.BlockSpec(memory_space=pltpu.SMEM)] * scalars + [pl.BlockSpec(memory_space=pltpu.VMEM)] * count


def shards(object_field, momentum, measured, illumination, slab_phase, offsets, entry_counts):
    rows = object_field.reshape(4, 8, W)
    momentum = momentum.reshape(4, 8, W)
    places = offsets[0, 0]
    right, left = (jnp.asarray(t) for t in tables(W))
    slab = jnp.stack([jnp.cos(slab_phase), jnp.sin(slab_phase)])
    dma = pltpu.SemaphoreType.DMA
    close = len(ROLES)
    window_shape = (4, 8, 4, 8, W)
    block_shape = (4, 2, 8, W)
    remote = functools.partial(
        pltpu.CompilerParams, has_side_effects=True, vmem_limit_bytes=VMEM_LIMIT
    )
    window = pl.pallas_call(
        gather_kernel,
        out_shape=jax.ShapeDtypeStruct(window_shape, f32),
        in_specs=specs(1, 1),
        out_specs=pl.BlockSpec(memory_space=pltpu.VMEM),
        scratch_shapes=[
            pltpu.VMEM((2, 2, *block_shape), f32),
            pltpu.VMEM((8, *block_shape), f32),
            dma((close,)),
            dma((close,)),
            dma((8,)),
            dma((16,)),
        ],
        compiler_params=remote(collective_id=0),
        name="gather_windows",
    )(places, rows)
    local = pltpu.CompilerParams(vmem_limit_bytes=VMEM_LIMIT)
    gradient = pl.pallas_call(
        gradient_kernel,
        out_shape=jax.ShapeDtypeStruct((4, W, W), f32),
        in_specs=specs(6, 2),
        out_specs=pl.BlockSpec(memory_space=pltpu.VMEM),
        compiler_params=local,
        name="window_gradient",
    )(places, entry_counts, window.reshape(4, W, W), measured[0, 0, 0], illumination, slab, right, left)
    new_rows, new_momentum, window = pl.pallas_call(
        return_kernel,
        out_shape=(
            jax.ShapeDtypeStruct((4, 8, W), f32),
            jax.ShapeDtypeStruct((4, 8, W), f32),
            jax.ShapeDtypeStruct(window_shape, f32),
        ),
        in_specs=specs(3, 1),
        out_specs=specs(3, 0),
        scratch_shapes=[
            pltpu.VMEM((8, *block_shape), f32),
            pltpu.VMEM((2, 2, *block_shape), f32),
            pltpu.VMEM((4, 4, 8, W), f32),
            pltpu.VMEM((4, 4, 8, W), f32),
            pltpu.VMEM((2, 2, *block_shape), f32),
            pltpu.VMEM((8, *block_shape), f32),
            dma((16,)),
            dma((8,)),
            dma((close,)),
            dma((close,)),
            dma((close,)),
            dma((close,)),
            dma((8,)),
            dma((16,)),
        ],
        compiler_params=remote(collective_id=1),
        name="return_gradients",
    )(places, rows, momentum, gradient.reshape(window_shape))
    amplitude = pl.pallas_call(
        predict_kernel,
        out_shape=jax.ShapeDtypeStruct((W, W), f32),
        in_specs=specs(5, 2),
        out_specs=pl.BlockSpec(memory_space=pltpu.VMEM),
        compiler_params=local,
        name="predict",
    )(places, entry_counts, window.reshape(4, W, W), illumination, slab, right, left)
    return (
        new_rows.reshape(2, 2, 8, W),
        new_momentum.reshape(2, 2, 8, W),
        amplitude[None, None, None],
    )


def solution(mesh):
    rows = P(None, None, ("ty", "pos"), "tx")
    slots = P("ty", "tx", "pos", None, None)
    return jax.shard_map(
        shards,
        mesh=mesh,
        in_specs=(rows, rows, slots, P(), P(), P("ty", "tx", None, None), P("ty", "tx")),
        out_specs=(rows, rows, slots),
        check_vma=False,
    )
```

time: 358 us -> 109 us (0.30); the launches traced: 354 us -> 109 us
  matrix products: 110 us -> 0 us
  Pallas kernels: 0 us -> 102 us
  starting transfers between devices: 71.4 us -> 0 us
  blocking collectives: 64.8 us -> 0 us
  waiting for transfers between devices: 42.8 us -> 0 us
  local copies, waits for them, and re-layouts: 38.6 us -> 5.71 us
  loops' own time: 15.3 us -> 0 us
  other arithmetic: 9.94 us -> 0.04 us
    dot_general x72 -> x0, matrix products: 110 us -> none  [matmul(): return jnp.dot(left, right, precision=HIGHEST)]
    pallas_call x0 -> x4, Pallas kernels: none -> 102 us  [the longest x1 50.6 us: shards(): pl.pallas_call(return_kernel, out_shape=(jax.ShapeDtypeStruct((4, 8, W),...]
    all_to_all x2 -> x0, blocking collectives: 64.8 us -> none  [the longest x1 32.7 us: sent_and_summed(): lax.all_to_all(cut_along(value, dim, devices), axis, 0, 0, tiled=True)]
    ppermute x12 -> x0, starting transfers between devices: 58.7 us -> none  [the longest x6 41.2 us: padded(): after = lax.ppermute(leading, axis, down)]
    all_to_all x1 -> x0, waiting for transfers between devices: 27.2 us -> none  [copy_for_each(): lax.all_to_all(jnp.broadcast_to(value[None], (devices, *value.shape)), ax...]
    ppermute x12 -> x0, waiting for transfers between devices: 15.6 us -> none  [the longest x6 11.8 us: padded(): after = lax.ppermute(leading, axis, down)]
    another operation x2 -> x0, loops' own time: 15.3 us -> none  [the longest x1 9.16 us: shards(): lax.fori_loop(zero, last_slot, accumulate, jnp.zeros((4, extent, extent),...]
    all_to_all x1 -> x0, starting transfers between devices: 12.7 us -> none  [copy_for_each(): lax.all_to_all(jnp.broadcast_to(value[None], (devices, *value.shape)), ax...]
  transfers between devices with their start and end apart: 13 -> 0, of which waited for: 7 -> 0; matrix products, arithmetic and copies ran while one was open for 2% -> 0% of each run, Pallas kernels for 0% -> 0%
where the time goes in v1:
time: 109 us
  Pallas kernels  102 us (94%)
  local copies, waits for them, and re-layouts  5.71 us (5%)
  between operations  1.56 us (1%)
    pallas_call x1, Pallas kernels, shards(): pl.pallas_call(return_kernel, out_shape=(jax.ShapeDtypeStruct((4, 8, W),...  50.6 us
    pallas_call x1, Pallas kernels, shards(): pl.pallas_call(gather_kernel, out_shape=jax.ShapeDtypeStruct(window_shape...  32.1 us
    pallas_call x1, Pallas kernels, shards(): pl.pallas_call(gradient_kernel, out_shape=jax.ShapeDtypeStruct((4, W, W),...  11.7 us
    pallas_call x1, Pallas kernels, shards(): pl.pallas_call(predict_kernel, out_shape=jax.ShapeDtypeStruct((W, W), f32...  7.08 us
    unnamed x18, local copies, waits for them, and re-layouts  3.05 us

profile of v1, /device:TPU:1, one launch (start us, length us, event | category | flops | bytes accessed | tf_op | source)
XLA Modules:
  0.0 108.9 jit_solution(5295809293567653917)
XLA Ops:
  0.6 0.0 copy-start
  0.6 0.0 copy-start.1
  0.7 0.0 copy-start.4
  1.5 0.8 copy.14.offsets
  2.3 1.9 %cosine_bitcast_fusion = (f32[1,256,256]{2,1,0:T(8,128)S(1)}, f32[1,256,256]{2,1,0:T(8,128)S(1)}) fusion(f32[256,256]{1,0:T(8,128)} %param.13), kind=kLoop, calls=%fused_computation.2 | loop fusion | bytes 786432 | tf_op jit(solution)/shard_map/stack | solution.py:463
  4.2 0.0 copy-start.5
  4.2 0.7 copy-done.5
  4.9 32.1 %gather_windows.1 = f32[4,8,4,8,256]{4,3,2,1,0:T(8,128)S(1)} custom-call(s32[32,2]{1,0:T(8,128)S(1)} %copy.14.offsets, f32[4,8,256]{2,1,0:T(8,128)S(1)} %bitcast.18), custom_call_target="tpu_custom_call" | custom-call | tf_op jit(solution)/shard_map/gather_windows/pallas_call | solution.py:471
  37.1 0.0 copy-done
  37.1 0.0 copy-done.1
  37.1 0.0 copy-done.4
  37.1 0.0 copy-start.2
  37.1 1.0 copy-done.2
  38.1 0.0 copy-start.6
  38.1 0.0 copy-start.7
  38.1 0.0 copy-start.3
  38.1 11.7 %window_gradient.1 = f32[4,256,256]{2,1,0:T(8,128)S(1)} custom-call(s32[32,2]{1,0:T(8,128)S(1)} %copy.14.offsets, s32[1,1]{1,0:T(1,128)S(6)} %copy.18.counts, f32[4,256,256]{2,1,0:T(8,128)S(1)} %bitcast.15, f32[256,256]{1,0:T(8,128)S(1)} %bitcast.17, f32[2,256,256]{2,1,0:T(8,128)S(1)} %copy-done.1, f32[2,256,256]{2,1,0:T(8,128)S(1)} %pad_maximum_fusion.slab, ...), custom_call_target="tpu_custom_call" | custom-call | tf_op jit(solution)/shard_map/window_gradient/pallas_call | solution.py:488
  49.9 0.0 copy-done.6
  49.9 0.0 copy-done.7
  49.9 50.6 %return_gradients.1 = (f32[4,8,256]{2,1,0:T(8,128)S(1)}, f32[4,8,256]{2,1,0:T(8,128)S(1)}, f32[4,8,4,8,256]{4,3,2,1,0:T(8,128)S(1)}) custom-call(s32[32,2]{1,0:T(8,128)S(1)} %copy.14.offsets, f32[4,8,256]{2,1,0:T(8,128)S(1)} %bitcast.19, f32[4,8,256]{2,1,0:T(8,128)S(1)} %bitcast.20, f32[4,8,4,8,256]{4,3,2,1,0:T(8,128)S(1)} %bitcast.14), custom_call_target="tpu_custom_call" | custom-call | tf_op jit(solution)/shard_map/return_gradients/pallas_call | solution.py:496
  100.5 0.0 copy-done.3
  100.6 7.1 %predict.1 = f32[256,256]{1,0:T(8,128)} custom-call(s32[32,2]{1,0:T(8,128)S(1)} %copy.14.offsets, s32[1,1]{1,0:T(1,128)S(6)} %copy.18.counts, f32[4,256,256]{2,1,0:T(8,128)S(1)} %bitcast.16, f32[2,256,256]{2,1,0:T(8,128)S(1)} %copy-done.1, f32[2,256,256]{2,1,0:T(8,128)S(1)} %pad_maximum_fusion.slab, bf16[2,512,256]{2,1,0:T(8,128)(2,1)S(1)} %copy-done.3, ...), custom_call_target="tpu_custom_call" | custom-call | tf_op jit(solution)/shard_map/predict/pallas_call | solution.py:524
  107.6 0.6 copy.19
  108.2 0.6 copy.20
  (1 shorter events, 0.0 us)
Async XLA Ops:
  0.6 36.4 %copy-start = (bf16[2,2,512,512]{3,2,1,0:T(8,128)(2,1)S(1)}, bf16[2,2,512,512]{3,2,1,0:T(8,128)(2,1)}, u32[]{:S(2)}) copy-start(bf16[2,2,512,512]{3,2,1,0:T(8,128)(2,1)} %constant.5.clone.left) | copy-start | bytes 6291460
  0.6 36.4 %copy-start.1 = (f32[2,256,256]{2,1,0:T(8,128)S(1)}, f32[2,256,256]{2,1,0:T(8,128)}, u32[]{:S(2)}) copy-start(f32[2,256,256]{2,1,0:T(8,128)} %illumination.3) | copy-start | bytes 1572868
  0.7 36.4 %copy-start.4 = (f32[1,1,1,256,256]{4,3,2,1,0:T(8,128)S(1)}, f32[1,1,1,256,256]{4,3,2,1,0:T(8,128)}, u32[]{:S(2)}) copy-start(f32[1,1,1,256,256]{4,3,2,1,0:T(8,128)} %param.11) | copy-start | bytes 786436
  4.2 0.8 copy-start.5
  37.1 1.0 copy-start.2
  38.1 11.7 %copy-start.6 = (f32[2,2,8,256]{3,2,1,0:T(8,128)S(1)}, f32[2,2,8,256]{3,2,1,0:T(8,128)}, u32[]{:S(2)}) copy-start(f32[2,2,8,256]{3,2,1,0:T(8,128)} %param.9) | copy-start | bytes 98308
  38.1 11.8 %copy-start.7 = (f32[2,2,8,256]{3,2,1,0:T(8,128)S(1)}, f32[2,2,8,256]{3,2,1,0:T(8,128)}, u32[]{:S(2)}) copy-start(f32[2,2,8,256]{3,2,1,0:T(8,128)} %param.10) | copy-start | bytes 98308
  38.1 62.4 %copy-start.3 = (bf16[2,512,256]{2,1,0:T(8,128)(2,1)S(1)}, bf16[2,512,256]{2,1,0:T(8,128)(2,1)}, u32[]{:S(2)}) copy-start(bf16[2,512,256]{2,1,0:T(8,128)(2,1)} %constant.4.clone.right) | copy-start | bytes 1572868

commit v2 on v1

v2 whole, which is shorter than its diff:
```python
import functools
import math

import jax
import jax.numpy as jnp
import numpy as np
from jax import lax
from jax.experimental import pallas as pl
from jax.experimental.pallas import tpu as pltpu
from jax.sharding import PartitionSpec as P

f32 = jnp.float32
bf16 = jnp.bfloat16
MESH = pl.DeviceIdType.MESH
magnitude_floor = 0.5
momentum_rate = 0.9
step_length = 0.05
W = 256
MARGIN = 64
ROLES = [(s, h, k) for s in range(2) for h in range(2) for k in range(3) if (s, h, k) != (0, 0, 0)]
VMEM_LIMIT = 48 * 1024 * 1024


def tables(length):
    indices = np.arange(length)
    angles = (indices[:, None] * indices[None, :] % length) * (2.0 * math.pi / length)
    c = np.cos(angles) / math.sqrt(length)
    s = np.sin(angles) / math.sqrt(length)

    def halves(value):
        value = value.astype(np.float32)
        high = value.astype(jnp.bfloat16)
        low = (value - high.astype(np.float32)).astype(jnp.bfloat16)
        return np.stack([high, low])

    right = halves(np.concatenate([c, s], axis=0))
    forward = halves(np.block([[c, s], [-s, c]]))
    inverse = halves(np.block([[c, -s], [s, c]]))
    return right, np.stack([forward, inverse])


def coordinates():
    ty = lax.axis_index("ty")
    tx = lax.axis_index("tx")
    pos = lax.axis_index("pos")
    return ty, tx, pos, pos // 8, (pos // 4) % 2, pos % 4


def peer(ty, tx, pos):
    return {"ty": ty, "tx": tx, "pos": pos}


def position(y, zh, x):
    return y * 8 + zh * 4 + x


def close_peer(role, outward):
    s, h, k = role
    ty, tx, pos, y, zh, x = coordinates()
    step = (0, 3, 1)[k] if outward else (0, 1, 3)[k]
    other_ty = 1 - ty if s else ty
    other_zh = 1 - zh if h else zh
    return other_ty, (tx + step) % 4, other_zh, position(y, other_zh, x)


def has_role(role, y_pair, tx_lower, tx_upper):
    s, h, k = role
    terms = ([y_pair] if s else []) + [[], [tx_lower], [tx_upper]][k]
    return functools.reduce(jnp.logical_and, terms) if terms else None


def when(condition, body):
    if condition is None:
        body()
    else:
        pl.when(condition)(body)


def enter():
    ty, tx, pos, y, zh, x = coordinates()
    barrier = pltpu.get_barrier_semaphore()
    outer = (y == 0) | (y == 3)
    for role in ROLES:
        other_ty, other_tx, _, other_pos = close_peer(role, True)

        def signal(other_ty=other_ty, other_tx=other_tx, other_pos=other_pos):
            pl.semaphore_signal(barrier, inc=1, device_id=peer(other_ty, other_tx, other_pos), device_id_type=MESH)

        when(has_role(role, outer, tx > 0, tx < 3), signal)
    near = jnp.where((tx == 0) | (tx == 3), 4, 6) * jnp.where(outer, 2, 1) - 1
    me = y * 4 + x
    small = (y % 2) * 4 + x

    def greet(start, count, modulus):
        def body(j, carry):
            t = (start + j) % modulus
            pl.semaphore_signal(
                barrier, inc=1, device_id=peer(ty, tx, position(t // 4, zh, t % 4)), device_id_type=MESH
            )
            return carry

        lax.fori_loop(0, count, body, 0)

    @pl.when(y < 2)
    def _():
        greet(me + 1, 15, 16)
        pl.semaphore_wait(barrier, near + 15)

    @pl.when(y >= 2)
    def _():
        greet(small, 8, 8)
        pl.semaphore_wait(barrier, near + 8)


def sibling_facts():
    ty, tx, pos, y, zh, x = coordinates()
    takes = ((ty == 0) & (y == 0)) | ((ty == 1) & (y == 3))
    gives = ((ty == 1) & (y == 0)) | ((ty == 0) & (y == 3))
    return takes, gives


def close_copy(index, role, piece, src, held, send_sem, recv_sem):
    ty, tx, pos, y, zh, x = coordinates()
    k = role[2]
    layers = pl.ds(2 * piece, 2)
    other_ty, other_tx, _, other_pos = close_peer(role, True)
    if k == 0:
        source, target = src.at[layers], held.at[ty, 0, layers, zh]
    else:
        lanes = pl.ds(128 * (k - 1), 128)
        source, target = src.at[layers, :, lanes], held.at[ty, 1, layers, zh, :, lanes]
    return pltpu.make_async_remote_copy(
        src_ref=source,
        dst_ref=target,
        send_sem=send_sem.at[piece, index],
        recv_sem=recv_sem.at[piece, index],
        device_id=peer(other_ty, other_tx, other_pos),
        device_id_type=MESH,
    )


def close_start(piece, src, held, send_sem, recv_sem):
    ty, tx, pos, y, zh, x = coordinates()
    takes, gives = sibling_facts()
    for index, role in enumerate(ROLES):
        copy = close_copy(index, role, piece, src, held, send_sem, recv_sem)
        when(has_role(role, gives, tx > 0, tx < 3), copy.start)
    for layer in (2 * piece, 2 * piece + 1):
        held[ty, 0, layer, zh] = src[layer]


def close_wait(piece, src, held, send_sem, recv_sem):
    ty, tx, pos, y, zh, x = coordinates()
    takes, gives = sibling_facts()
    for index, role in enumerate(ROLES):
        copy = close_copy(index, role, piece, src, held, send_sem, recv_sem)
        when(has_role(role, takes, tx < 3, tx > 0), copy.wait_recv)


def close_drain(piece, src, held, send_sem, recv_sem):
    ty, tx, pos, y, zh, x = coordinates()
    takes, gives = sibling_facts()
    for index, role in enumerate(ROLES):
        copy = close_copy(index, role, piece, src, held, send_sem, recv_sem)
        when(has_role(role, gives, tx > 0, tx < 3), copy.wait_send)


def clear_missing(held):
    ty, tx, pos, y, zh, x = coordinates()
    takes, gives = sibling_facts()
    nothing = jnp.zeros((4, 2, 8, 128), f32)

    @pl.when(jnp.logical_not(takes))
    def _():
        for kind in range(2):
            held[1 - ty, kind] = jnp.zeros((4, 2, 8, W), f32)

    @pl.when(tx == 3)
    def _():
        for core in range(2):
            held[core, 1, :, :, :, 0:128] = nothing

    @pl.when(tx == 0)
    def _():
        for core in range(2):
            held[core, 1, :, :, :, 128:256] = nothing


def row_swap(row_start):
    ty, tx, pos, y, zh, x = coordinates()
    shape = (2, 8, W)
    row = (
        y * 64
        + x * 8
        + lax.broadcasted_iota(jnp.int32, shape, 0) * 32
        + lax.broadcasted_iota(jnp.int32, shape, 1)
    )
    return ((row < MARGIN) & (row_start > row + MARGIN)) | ((row >= 192) & (row > row_start + 191))


def column_swap(column_start):
    column = lax.broadcasted_iota(jnp.int32, (2, 8, W), 2)
    return ((column < MARGIN) & (column_start > column + MARGIN)) | (
        (column >= 192) & (column > column_start + 191)
    )


def far_copy(j, piece, blocks, window, send_sem, recv_sem):
    ty, tx, pos, y, zh, x = coordinates()
    t = ((y % 2) * 4 + x + j) % 8
    return pltpu.make_async_remote_copy(
        src_ref=blocks.at[piece, j],
        dst_ref=window.at[pl.ds(2 * piece, 2), pl.ds(2 * y, 2), x],
        send_sem=send_sem.at[piece, j],
        recv_sem=recv_sem.at[piece, y * 4 + x],
        device_id=peer(ty, tx, position(t // 4, zh, t % 4)),
        device_id_type=MESH,
    )


def far_start(piece, offsets, held, blocks, window, send_sem, recv_sem):
    ty, tx, pos, y, zh, x = coordinates()
    for j in range(8):
        t = ((y % 2) * 4 + x + j) % 8
        target = position(t // 4, zh, t % 4)
        swap_rows = row_swap(offsets[target, 0])
        swap_columns = column_swap(offsets[target, 1])
        for part in range(2):
            layer = 2 * piece + part
            own = jnp.where(swap_columns, held[ty, 1, layer], held[ty, 0, layer])
            sibling = jnp.where(swap_columns, held[1 - ty, 1, layer], held[1 - ty, 0, layer])
            blocks[piece, j, part] = jnp.where(swap_rows, sibling, own)
        if j == 0:

            @pl.when(y >= 2)
            def _():
                far_copy(0, piece, blocks, window, send_sem, recv_sem).start()

            @pl.when(y < 2)
            def _():
                for part in range(2):
                    window[2 * piece + part, pl.ds(2 * y, 2), x] = blocks[piece, 0, part]

        else:
            far_copy(j, piece, blocks, window, send_sem, recv_sem).start()


def far_wait(piece, blocks, window, send_sem, recv_sem):
    ty, tx, pos, y, zh, x = coordinates()

    def arrive(j, carry):
        s = (y * 4 + x + j) % 16
        pltpu.make_async_remote_copy(
            src_ref=blocks.at[piece, 0],
            dst_ref=window.at[pl.ds(2 * piece, 2), pl.ds(2 * (s // 4), 2), s % 4],
            send_sem=send_sem.at[piece, 0],
            recv_sem=recv_sem.at[piece, s],
            device_id=peer(ty, tx, position(s // 4, zh, s % 4)),
            device_id_type=MESH,
        ).wait_recv()
        return carry

    lax.fori_loop(1, 16, arrive, 0)


def far_drain(piece, blocks, window, send_sem, recv_sem):
    ty, tx, pos, y, zh, x = coordinates()

    @pl.when(y >= 2)
    def _():
        far_copy(0, piece, blocks, window, send_sem, recv_sem).wait_send()

    for j in range(1, 8):
        far_copy(j, piece, blocks, window, send_sem, recv_sem).wait_send()


def return_copy(j, piece, gradient, arrived, send_sem, recv_sem):
    ty, tx, pos, y, zh, x = coordinates()
    t = (y * 4 + x + j) % 16
    return pltpu.make_async_remote_copy(
        src_ref=gradient.at[pl.ds(2 * piece, 2), pl.ds(2 * (t // 4), 2), t % 4],
        dst_ref=arrived.at[piece, (y % 2) * 4 + x],
        send_sem=send_sem.at[piece, j],
        recv_sem=recv_sem.at[piece, (y % 2) * 4 + x],
        device_id=peer(ty, tx, position(t // 4, zh, t % 4)),
        device_id_type=MESH,
    )


def return_start(piece, gradient, arrived, send_sem, recv_sem):
    ty, tx, pos, y, zh, x = coordinates()

    def leave(j, carry):
        return_copy(j, piece, gradient, arrived, send_sem, recv_sem).start()
        return carry

    lax.fori_loop(1, 16, leave, 0)
    for part in range(2):
        arrived[piece, (y % 2) * 4 + x, part] = gradient[2 * piece + part, pl.ds(2 * y, 2), x]


def return_wait(piece, gradient, arrived, send_sem, recv_sem):
    ty, tx, pos, y, zh, x = coordinates()
    base = (y % 2) * 4 + x

    def wait_for(s):
        pltpu.make_async_remote_copy(
            src_ref=gradient.at[pl.ds(2 * piece, 2), pl.ds(0, 2), 0],
            dst_ref=arrived.at[piece, s],
            send_sem=send_sem.at[piece, 0],
            recv_sem=recv_sem.at[piece, s],
            device_id=peer(ty, tx, position(s // 4, zh, s % 4)),
            device_id_type=MESH,
        ).wait_recv()

    @pl.when(y >= 2)
    def _():
        wait_for(base)

    for j in range(1, 8):
        wait_for((base + j) % 8)


def return_drain(piece, gradient, arrived, send_sem, recv_sem):
    def left(j, carry):
        return_copy(j, piece, gradient, arrived, send_sem, recv_sem).wait_send()
        return carry

    lax.fori_loop(1, 16, left, 0)


def add_returned(piece, offsets, arrived, sums):
    ty, tx, pos, y, zh, x = coordinates()
    swaps = []
    for j in range(8):
        target = position(j // 4, zh, j % 4)
        swaps.append((row_swap(offsets[target, 0]), column_swap(offsets[target, 1])))
    for part in range(2):
        layer = 2 * piece + part
        own = jnp.zeros((2, 8, W), f32)
        own_side, sibling, sibling_side = own, own, own
        for j in range(8):
            swap_rows, swap_columns = swaps[j]
            block = arrived[piece, j, part]
            mine = jnp.where(swap_rows, 0.0, block)
            theirs = jnp.where(swap_rows, block, 0.0)
            own = own + jnp.where(swap_columns, 0.0, mine)
            own_side = own_side + jnp.where(swap_columns, mine, 0.0)
            sibling = sibling + jnp.where(swap_columns, 0.0, theirs)
            sibling_side = sibling_side + jnp.where(swap_columns, theirs, 0.0)
        sums[ty, 0, layer] = own
        sums[ty, 1, layer] = own_side
        sums[1 - ty, 0, layer] = sibling
        sums[1 - ty, 1, layer] = sibling_side


def sum_copy(index, role, piece, sums, parts_own, parts_side, send_sem, recv_sem):
    s, h, k = role
    layers = pl.ds(2 * piece, 2)
    other_ty, other_tx, other_zh, other_pos = close_peer(role, False)
    if k == 0:
        source, target = sums.at[other_ty, 0, layers, other_zh], parts_own.at[2 * s + h, layers]
    else:
        lanes = pl.ds(128 * (k - 1), 128)
        source = sums.at[other_ty, 1, layers, other_zh, :, lanes]
        target = parts_side.at[2 * s + h, layers, :, lanes]
    return pltpu.make_async_remote_copy(
        src_ref=source,
        dst_ref=target,
        send_sem=send_sem.at[piece, index],
        recv_sem=recv_sem.at[piece, index],
        device_id=peer(other_ty, other_tx, other_pos),
        device_id_type=MESH,
    )


def sum_each(piece, action, *refs):
    ty, tx, pos, y, zh, x = coordinates()
    takes, gives = sibling_facts()
    for index, role in enumerate(ROLES):
        copy = sum_copy(index, role, piece, *refs)
        if action == "recv":
            when(has_role(role, gives, tx > 0, tx < 3), copy.wait_recv)
        else:
            act = copy.start if action == "start" else copy.wait_send
            when(has_role(role, takes, tx < 3, tx > 0), act)


def clear_parts(parts_own, parts_side):
    ty, tx, pos, y, zh, x = coordinates()
    takes, gives = sibling_facts()
    nothing = jnp.zeros((4, 8, 128), f32)

    @pl.when(jnp.logical_not(gives))
    def _():
        for part in (2, 3):
            parts_own[part] = jnp.zeros((4, 8, W), f32)
            parts_side[part] = jnp.zeros((4, 8, W), f32)

    @pl.when(tx == 0)
    def _():
        for part in range(4):
            parts_side[part, :, :, 0:128] = nothing

    @pl.when(tx == 3)
    def _():
        for part in range(4):
            parts_side[part, :, :, 128:256] = nothing


def split(value):
    high = value.astype(bf16)
    return high, (value - high.astype(f32)).astype(bf16)


def product(left, right):
    return jnp.dot(left, right, preferred_element_type=f32)


def transform(real_part, imag_part, right, left, inverse):
    def stacked(r, i):
        if inverse:
            return jnp.concatenate([jnp.concatenate([r, -i], 1), jnp.concatenate([i, r], 1)], 0)
        return jnp.concatenate([jnp.concatenate([r, i], 1), jnp.concatenate([i, -r], 1)], 0)

    real_high, real_low = split(real_part)
    imag_high, imag_low = split(imag_part)
    high = stacked(real_high, imag_high)
    low = stacked(real_low, imag_low)
    middle = product(high, right[0]) + product(low, right[0]) + product(high, right[1])
    high, low = split(middle)
    which = 1 if inverse else 0
    result = product(left[which, 0], high) + product(left[which, 0], low) + product(left[which, 1], high)
    return result[:W], result[W:]


def complex_product(first_real, first_imag, second_real, second_imag):
    return (
        first_real * second_real - first_imag * second_imag,
        first_real * second_imag + first_imag * second_real,
    )


def shifted_probe(offsets, illumination):
    pos = lax.axis_index("pos")
    down = (offsets[pos, 0] + 192) % 256
    across = (offsets[pos, 1] + 192) % 256
    return [pltpu.roll(pltpu.roll(illumination[part], down, 0), across, 1) for part in range(2)]


def layer_of(window, layer):
    return window[layer].reshape(W, W)


def between_field(window, probe, slab, right, left):
    entering = complex_product(probe[0], probe[1], layer_of(window, 0), layer_of(window, 1))
    spectrum = transform(entering[0], entering[1], right, left, False)
    spectrum = complex_product(spectrum[0], spectrum[1], slab[0], slab[1])
    return transform(spectrum[0], spectrum[1], right, left, True)


def farfield_of(between, window, right, left):
    leaving = complex_product(between[0], between[1], layer_of(window, 2), layer_of(window, 3))
    return transform(leaving[0], leaving[1], right, left, False)


def kernel(
    offsets,
    counts,
    rows,
    momentum,
    measured_hbm,
    illumination_hbm,
    phase_hbm,
    right_hbm,
    left_hbm,
    new_rows,
    new_momentum,
    amplitude,
    measured,
    illumination,
    phase,
    right,
    left,
    probe,
    slab,
    between_kept,
    held_first,
    held_second,
    blocks_first,
    blocks_second,
    window_first,
    window_second,
    gradient,
    arrived,
    sums,
    parts_own,
    parts_side,
    local_sem,
    close_send_first,
    close_recv_first,
    close_send_second,
    close_recv_second,
    far_send_first,
    far_recv_first,
    far_send_second,
    far_recv_second,
    return_send,
    return_recv,
    sum_send,
    sum_recv,
):
    ty, tx, pos, y, zh, x = coordinates()
    loads = [
        pltpu.make_async_copy(source, target, local_sem.at[n])
        for n, (source, target) in enumerate(
            (
                (phase_hbm, phase),
                (illumination_hbm, illumination),
                (right_hbm, right),
                (left_hbm, left),
                (measured_hbm, measured),
            )
        )
    ]

    @pl.when(y < 2)
    def _():
        for load in loads:
            load.start()

    clear_missing(held_first)
    clear_missing(held_second)
    clear_parts(parts_own, parts_side)
    enter()
    close_first = (rows, held_first, close_send_first, close_recv_first)
    close_second = (new_rows, held_second, close_send_second, close_recv_second)
    far_first = (blocks_first, window_first, far_send_first, far_recv_first)
    far_second = (blocks_second, window_second, far_send_second, far_recv_second)
    returned = (gradient, arrived, return_send, return_recv)
    summed = (sums, parts_own, parts_side, sum_send, sum_recv)
    for piece in (0, 1):
        close_start(piece, *close_first)
    for piece in (0, 1):
        close_wait(piece, *close_first)
        far_start(piece, offsets, held_first, *far_first)
    live = jnp.where(pos < counts[0, 0], 1.0, 0.0)

    @pl.when(y < 2)
    def _():
        for load in loads:
            load.wait()
        slab[0] = jnp.cos(phase[...])
        slab[1] = jnp.sin(phase[...])
        shifted = shifted_probe(offsets, illumination)
        probe[0] = shifted[0]
        probe[1] = shifted[1]
        far_wait(0, *far_first)
        between = between_field(window_first, probe, slab, right, left)
        between_kept[0] = between[0]
        between_kept[1] = between[1]
        far_wait(1, *far_first)
        farfield = farfield_of(between, window_first, right, left)
        magnitude = jnp.sqrt(farfield[0] * farfield[0] + farfield[1] * farfield[1])
        keeping = (1.0 - measured[...] / jnp.maximum(magnitude, magnitude_floor)) * live
        backward = transform(farfield[0] * keeping, farfield[1] * keeping, right, left, True)
        grad_second = complex_product(between_kept[0], -between_kept[1], backward[0], backward[1])
        gradient[2] = grad_second[0].reshape(8, 4, 8, W)
        gradient[3] = grad_second[1].reshape(8, 4, 8, W)
        return_start(1, *returned)
        toward = complex_product(layer_of(window_first, 2), -layer_of(window_first, 3), backward[0], backward[1])
        spectrum = transform(toward[0], toward[1], right, left, False)
        spectrum = complex_product(spectrum[0], spectrum[1], slab[0], -slab[1])
        incoming = transform(spectrum[0], spectrum[1], right, left, True)
        grad_first = complex_product(probe[0], -probe[1], incoming[0], incoming[1])
        gradient[0] = grad_first[0].reshape(8, 4, 8, W)
        gradient[1] = grad_first[1].reshape(8, 4, 8, W)
        return_start(0, *returned)

    for piece in (1, 0):
        return_wait(piece, *returned)
        add_returned(piece, offsets, arrived, sums)
        sum_each(piece, "start", *summed)
        sum_each(piece, "recv", *summed)
        for layer in (2 * piece, 2 * piece + 1):
            total = sums[ty, 0, layer, zh]
            for part in range(4):
                if part:
                    total = total + parts_own[part, layer]
                total = total + parts_side[part, layer]
            velocity = momentum_rate * momentum[layer] + total
            new_momentum[layer] = velocity
            new_rows[layer] = rows[layer] - step_length * velocity
        close_start(piece, *close_second)
        close_wait(piece, *close_second)
        far_start(piece, offsets, held_second, *far_second)

    @pl.when(y < 2)
    def _():
        far_wait(0, *far_second)
        between = between_field(window_second, probe, slab, right, left)
        far_wait(1, *far_second)
        farfield = farfield_of(between, window_second, right, left)
        amplitude[...] = jnp.sqrt(farfield[0] * farfield[0] + farfield[1] * farfield[1]) * live

    @pl.when(y >= 2)
    def _():
        amplitude[...] = jnp.zeros_like(amplitude)

    for piece in (0, 1):
        close_drain(piece, *close_first)
        close_drain(piece, *close_second)
        far_drain(piece, *far_first)
        far_drain(piece, *far_second)
        sum_each(piece, "sent", *summed)

    @pl.when(y < 2)
    def _():
        for piece in (0, 1):
            return_drain(piece, *returned)


def shards(object_field, momentum, measured, illumination, slab_phase, offsets, entry_counts):
    rows = object_field.reshape(4, 8, W)
    right, left = (jnp.asarray(t) for t in tables(W))
    dma = pltpu.SemaphoreType.DMA
    close = len(ROLES)
    window_shape = (4, 8, 4, 8, W)
    held_shape = (2, 2, 4, 2, 8, W)
    blocks_shape = (2, 8, 2, 2, 8, W)
    field = (2, W, W)
    vmem = pl.BlockSpec(memory_space=pltpu.VMEM)
    smem = pl.BlockSpec(memory_space=pltpu.SMEM)
    remain = pl.BlockSpec(memory_space=pl.ANY)
    new_rows, new_momentum, amplitude = pl.pallas_call(
        kernel,
        out_shape=(
            jax.ShapeDtypeStruct((4, 8, W), f32),
            jax.ShapeDtypeStruct((4, 8, W), f32),
            jax.ShapeDtypeStruct((W, W), f32),
        ),
        in_specs=[smem, smem, vmem, vmem, remain, remain, remain, remain, remain],
        out_specs=[vmem, vmem, vmem],
        scratch_shapes=[
            pltpu.VMEM((W, W), f32),
            pltpu.VMEM(field, f32),
            pltpu.VMEM((W, W), f32),
            pltpu.VMEM(right.shape, bf16),
            pltpu.VMEM(left.shape, bf16),
            pltpu.VMEM(field, f32),
            pltpu.VMEM(field, f32),
            pltpu.VMEM(field, f32),
            pltpu.VMEM(held_shape, f32),
            pltpu.VMEM(held_shape, f32),
            pltpu.VMEM(blocks_shape, f32),
            pltpu.VMEM(blocks_shape, f32),
            pltpu.VMEM(window_shape, f32),
            pltpu.VMEM(window_shape, f32),
            pltpu.VMEM(window_shape, f32),
            pltpu.VMEM(blocks_shape, f32),
            pltpu.VMEM(held_shape, f32),
            pltpu.VMEM((4, 4, 8, W), f32),
            pltpu.VMEM((4, 4, 8, W), f32),
            dma((5,)),
            dma((2, close)),
            dma((2, close)),
            dma((2, close)),
            dma((2, close)),
            dma((2, 8)),
            dma((2, 16)),
            dma((2, 8)),
            dma((2, 16)),
            dma((2, 16)),
            dma((2, 8)),
            dma((2, close)),
            dma((2, close)),
        ],
        compiler_params=pltpu.CompilerParams(
            has_side_effects=True, vmem_limit_bytes=VMEM_LIMIT, collective_id=0
        ),
        name="iterate",
    )(
        offsets[0, 0],
        entry_counts,
        rows,
        momentum.reshape(4, 8, W),
        measured[0, 0, 0],
        illumination,
        slab_phase,
        right,
        left,
    )
    return (
        new_rows.reshape(2, 2, 8, W),
        new_momentum.reshape(2, 2, 8, W),
        amplitude[None, None, None],
    )


def solution(mesh):
    rows = P(None, None, ("ty", "pos"), "tx")
    slots = P("ty", "tx", "pos", None, None)
    return jax.shard_map(
        shards,
        mesh=mesh,
        in_specs=(rows, rows, slots, P(), P(), P("ty", "tx", None, None), P("ty", "tx")),
        out_specs=(rows, rows, slots),
        check_vma=False,
    )
```

time: 109 us -> 91.3 us (0.84)
  Pallas kernels: 102 us -> 79.1 us
  local copies, waits for them, and re-layouts: 5.71 us -> 9.78 us
    pallas_call x4 -> x1, Pallas kernels: 102 us -> 79.1 us  [shards(): pl.pallas_call(kernel, out_shape=(jax.ShapeDtypeStruct((4, 8, W), f32), j...]
    unnamed x18 -> x17, local copies, waits for them, and re-layouts: 3.05 us -> 9.02 us
    another operation x1 -> x0, local copies, waits for them, and re-layouts: 1.85 us -> none  [shards(): slab = jnp.stack([jnp.cos(slab_phase), jnp.sin(slab_phase)])]
where the time goes in v2:
time: 91.3 us; the launch traced here: 90.2 us
  Pallas kernels  79.1 us (87%)
  local copies, waits for them, and re-layouts  9.78 us (11%)
  between operations  1.29 us (1%)
    pallas_call x1, Pallas kernels, shards(): pl.pallas_call(kernel, out_shape=(jax.ShapeDtypeStruct((4, 8, W), f32), j...  79.1 us
    unnamed x17, local copies, waits for them, and re-layouts  9.02 us

profile of v2, /device:TPU:1, one launch (start us, length us, event | category | flops | bytes accessed | tf_op | source)
XLA Modules:
  0.0 90.2 jit_solution(11643554645117061492)
XLA Ops:
  1.3 0.8 copy.12.offsets
  2.0 0.0 copy-start
  2.0 1.6 %copy-done = bf16[2,2,512,512]{3,2,1,0:T(8,128)(2,1)S(1)} copy-done((bf16[2,2,512,512]{3,2,1,0:T(8,128)(2,1)S(1)}, bf16[2,2,512,512]{3,2,1,0:T(8,128)(2,1)}, u32[]{:S(2)}) %copy-start) | copy-done | bytes 2097176
  3.6 0.0 copy-start.1
  3.6 1.0 %copy-done.1 = f32[2,256,256]{2,1,0:T(8,128)S(1)} copy-done((f32[2,256,256]{2,1,0:T(8,128)S(1)}, f32[2,256,256]{2,1,0:T(8,128)}, u32[]{:S(2)}) %copy-start.1) | copy-done | bytes 524312
  4.7 0.0 copy-start.2
  4.7 1.0 %copy-done.2 = bf16[2,512,256]{2,1,0:T(8,128)(2,1)S(1)} copy-done((bf16[2,512,256]{2,1,0:T(8,128)(2,1)S(1)}, bf16[2,512,256]{2,1,0:T(8,128)(2,1)}, u32[]{:S(2)}) %copy-start.2) | copy-done | bytes 524312
  5.7 0.0 copy-start.3
  5.7 0.9 %copy-done.3 = f32[1,1,1,256,256]{4,3,2,1,0:T(8,128)S(1)} copy-done((f32[1,1,1,256,256]{4,3,2,1,0:T(8,128)S(1)}, f32[1,1,1,256,256]{4,3,2,1,0:T(8,128)}, u32[]{:S(2)}) %copy-start.3) | copy-done | bytes 262168
  6.7 0.0 copy-start.4
  6.7 0.9 %copy-done.4 = f32[256,256]{1,0:T(8,128)S(1)} copy-done((f32[256,256]{1,0:T(8,128)S(1)}, f32[256,256]{1,0:T(8,128)}, u32[]{:S(2)}) %copy-start.4) | copy-done | bytes 262168
  7.6 0.0 copy-start.5
  7.6 0.8 copy-done.5
  8.4 0.0 copy-start.6
  8.4 0.8 copy-done.6
  9.1 79.1 %iterate.1 = (f32[4,8,256]{2,1,0:T(8,128)S(1)}, f32[4,8,256]{2,1,0:T(8,128)S(1)}, f32[256,256]{1,0:T(8,128)S(1)}) custom-call(s32[32,2]{1,0:T(8,128)S(1)} %copy.12.offsets, s32[1,1]{1,0:T(1,128)S(6)} %copy.16.counts, f32[4,8,256]{2,1,0:T(8,128)S(1)} %bitcast.9, f32[4,8,256]{2,1,0:T(8,128)S(1)} %bitcast.10, f32[256,256]{1,0:T(8,128)S(1)} %bitcast.7, ...), custom_call_target="tpu_custom_call" | custom-call | tf_op jit(solution)/shard_map/iterate/pallas_call | solution.py:635
  88.3 0.6 copy.17
  88.9 0.6 copy.18
  89.5 0.7 copy.19
Async XLA Ops:
  2.0 1.6 %copy-start = (bf16[2,2,512,512]{3,2,1,0:T(8,128)(2,1)S(1)}, bf16[2,2,512,512]{3,2,1,0:T(8,128)(2,1)}, u32[]{:S(2)}) copy-start(bf16[2,2,512,512]{3,2,1,0:T(8,128)(2,1)} %constant.5.clone.left_hbm) | copy-start | bytes 6291460
  3.6 1.0 %copy-start.1 = (f32[2,256,256]{2,1,0:T(8,128)S(1)}, f32[2,256,256]{2,1,0:T(8,128)}, u32[]{:S(2)}) copy-start(f32[2,256,256]{2,1,0:T(8,128)} %illumination_hbm.1) | copy-start | bytes 1572868
  4.7 1.0 %copy-start.2 = (bf16[2,512,256]{2,1,0:T(8,128)(2,1)S(1)}, bf16[2,512,256]{2,1,0:T(8,128)(2,1)}, u32[]{:S(2)}) copy-start(bf16[2,512,256]{2,1,0:T(8,128)(2,1)} %constant.4.clone.right_hbm) | copy-start | bytes 1572868
  5.7 0.9 %copy-start.3 = (f32[1,1,1,256,256]{4,3,2,1,0:T(8,128)S(1)}, f32[1,1,1,256,256]{4,3,2,1,0:T(8,128)}, u32[]{:S(2)}) copy-start(f32[1,1,1,256,256]{4,3,2,1,0:T(8,128)} %param.11) | copy-start | bytes 786436
  6.7 0.9 %copy-start.4 = (f32[256,256]{1,0:T(8,128)S(1)}, f32[256,256]{1,0:T(8,128)}, u32[]{:S(2)}) copy-start(f32[256,256]{1,0:T(8,128)} %phase_hbm.1) | copy-start | bytes 786436
  7.6 0.8 copy-start.5
  8.4 0.8 copy-start.6

commit v3 on v2

--- a/solution.py
+++ b/solution.py
@@ -18,14 +18,12 @@
 W = 256
 MARGIN = 64
 ROLES = [(s, h, k) for s in range(2) for h in range(2) for k in range(3) if (s, h, k) != (0, 0, 0)]
-VMEM_LIMIT = 48 * 1024 * 1024
+VMEM_LIMIT = 60 * 1024 * 1024
 
 
 def tables(length):
-    indices = np.arange(length)
-    angles = (indices[:, None] * indices[None, :] % length) * (2.0 * math.pi / length)
-    c = np.cos(angles) / math.sqrt(length)
-    s = np.sin(angles) / math.sqrt(length)
+    half = length // 2
+    place = np.arange(half)
 
     def halves(value):
         value = value.astype(np.float32)
@@ -33,10 +31,21 @@
         low = (value - high.astype(np.float32)).astype(jnp.bfloat16)
         return np.stack([high, low])
 
-    right = halves(np.concatenate([c, s], axis=0))
-    forward = halves(np.block([[c, s], [-s, c]]))
-    inverse = halves(np.block([[c, -s], [s, c]]))
-    return right, np.stack([forward, inverse])
+    right = []
+    for direction in (-1.0, 1.0):
+        for odd in (0, 1):
+            turns = (place[:, None] * (2 * place[None, :] + odd)) % length
+            if direction > 0:
+                turns = turns.T
+            angles = turns * (direction * 2.0 * math.pi / length)
+            c = np.cos(angles) / math.sqrt(length)
+            s = np.sin(angles) / math.sqrt(length)
+            right.append(halves(np.block([[c, s], [-s, c]])))
+    right = np.stack(right).reshape(2, 2, 2, length, length)
+    left = right.swapaxes(3, 4)
+    order = np.zeros((length, length))
+    order[np.arange(length), np.concatenate([2 * place, 2 * place + 1])] = 1.0
+    return right, np.ascontiguousarray(left), np.stack([order, order.T]).astype(jnp.bfloat16)
 
 
 def coordinates():
@@ -101,15 +110,19 @@
 
         lax.fori_loop(0, count, body, 0)
 
-    @pl.when(y < 2)
+    @pl.when((y < 2) | (ty == 1))
     def _():
         greet(me + 1, 15, 16)
         pl.semaphore_wait(barrier, near + 15)
 
-    @pl.when(y >= 2)
+    @pl.when((y >= 2) & (ty == 0))
     def _():
         greet(small, 8, 8)
         pl.semaphore_wait(barrier, near + 8)
+
+
+def turned_row(y, turned):
+    return y + turned * (3 - 2 * y)
 
 
 def sibling_facts():
@@ -142,17 +155,21 @@
 def close_start(piece, src, held, send_sem, recv_sem):
     ty, tx, pos, y, zh, x = coordinates()
     takes, gives = sibling_facts()
-    for index, role in enumerate(ROLES):
-        copy = close_copy(index, role, piece, src, held, send_sem, recv_sem)
-        when(has_role(role, gives, tx > 0, tx < 3), copy.start)
+    for half in (1, 0):
+        for index, role in enumerate(ROLES):
+            if role[1] == half:
+                copy = close_copy(index, role, piece, src, held, send_sem, recv_sem)
+                when(has_role(role, gives, tx > 0, tx < 3), copy.start)
     for layer in (2 * piece, 2 * piece + 1):
         held[ty, 0, layer, zh] = src[layer]
 
 
-def close_wait(piece, src, held, send_sem, recv_sem):
+def close_wait(piece, half, src, held, send_sem, recv_sem):
     ty, tx, pos, y, zh, x = coordinates()
     takes, gives = sibling_facts()
     for index, role in enumerate(ROLES):
+        if role[1] != half:
+            continue
         copy = close_copy(index, role, piece, src, held, send_sem, recv_sem)
         when(has_role(role, takes, tx < 3, tx > 0), copy.wait_recv)
 
@@ -186,63 +203,65 @@
             held[core, 1, :, :, :, 128:256] = nothing
 
 
-def row_swap(row_start):
-    ty, tx, pos, y, zh, x = coordinates()
-    shape = (2, 8, W)
-    row = (
-        y * 64
-        + x * 8
-        + lax.broadcasted_iota(jnp.int32, shape, 0) * 32
-        + lax.broadcasted_iota(jnp.int32, shape, 1)
-    )
+def row_swap(row_start, zh):
+    ty, tx, pos, y, _, x = coordinates()
+    row = y * 64 + zh * 32 + x * 8 + lax.broadcasted_iota(jnp.int32, (8, W), 0)
     return ((row < MARGIN) & (row_start > row + MARGIN)) | ((row >= 192) & (row > row_start + 191))
 
 
 def column_swap(column_start):
-    column = lax.broadcasted_iota(jnp.int32, (2, 8, W), 2)
+    column = lax.broadcasted_iota(jnp.int32, (8, W), 1)
     return ((column < MARGIN) & (column_start > column + MARGIN)) | (
         (column >= 192) & (column > column_start + 191)
     )
 
 
-def far_copy(j, piece, blocks, window, send_sem, recv_sem):
-    ty, tx, pos, y, zh, x = coordinates()
-    t = ((y % 2) * 4 + x + j) % 8
+def far_copy(j, piece, rows, turned, blocks, window, send_sem, recv_sem):
+    ty, tx, pos, y, zh, x = coordinates()
+    t = ((turned_row(y, turned) % 2) * 4 + x + j) % 8
+    layers = pl.ds(2 * piece, 2)
+    if rows is None:
+        source, target = blocks.at[piece, j], window.at[layers, pl.ds(2 * y, 2), x]
+    else:
+        source, target = blocks.at[piece, j, :, rows], window.at[layers, 2 * y + rows, x]
     return pltpu.make_async_remote_copy(
-        src_ref=blocks.at[piece, j],
-        dst_ref=window.at[pl.ds(2 * piece, 2), pl.ds(2 * y, 2), x],
+        src_ref=source,
+        dst_ref=target,
         send_sem=send_sem.at[piece, j],
         recv_sem=recv_sem.at[piece, y * 4 + x],
-        device_id=peer(ty, tx, position(t // 4, zh, t % 4)),
+        device_id=peer(ty, tx, position(turned_row(t // 4, turned), zh, t % 4)),
         device_id_type=MESH,
     )
 
 
-def far_start(piece, offsets, held, blocks, window, send_sem, recv_sem):
-    ty, tx, pos, y, zh, x = coordinates()
+def far_start(piece, half, turned, offsets, held, *far):
+    ty, tx, pos, y, zh, x = coordinates()
+    blocks, window = far[:2]
+    rows = 1 - zh if half else zh
+    slot_row = turned_row(y, turned)
     for j in range(8):
-        t = ((y % 2) * 4 + x + j) % 8
+        t = ((slot_row % 2) * 4 + x + j) % 8
         target = position(t // 4, zh, t % 4)
-        swap_rows = row_swap(offsets[target, 0])
-        swap_columns = column_swap(offsets[target, 1])
+        swap_rows = row_swap(offsets[0, target], rows)
+        swap_columns = column_swap(offsets[1, target])
         for part in range(2):
             layer = 2 * piece + part
-            own = jnp.where(swap_columns, held[ty, 1, layer], held[ty, 0, layer])
-            sibling = jnp.where(swap_columns, held[1 - ty, 1, layer], held[1 - ty, 0, layer])
-            blocks[piece, j, part] = jnp.where(swap_rows, sibling, own)
+            own = jnp.where(swap_columns, held[ty, 1, layer, rows], held[ty, 0, layer, rows])
+            sibling = jnp.where(swap_columns, held[1 - ty, 1, layer, rows], held[1 - ty, 0, layer, rows])
+            blocks[piece, j, part, rows] = jnp.where(swap_rows, sibling, own)
         if j == 0:
 
-            @pl.when(y >= 2)
+            @pl.when(slot_row >= 2)
             def _():
-                far_copy(0, piece, blocks, window, send_sem, recv_sem).start()
-
-            @pl.when(y < 2)
+                far_copy(0, piece, rows, turned, *far).start()
+
+            @pl.when(slot_row < 2)
             def _():
                 for part in range(2):
-                    window[2 * piece + part, pl.ds(2 * y, 2), x] = blocks[piece, 0, part]
+                    window[2 * piece + part, 2 * y + rows, x] = blocks[piece, 0, part, rows]
 
         else:
-            far_copy(j, piece, blocks, window, send_sem, recv_sem).start()
+            far_copy(j, piece, rows, turned, *far).start()
 
 
 def far_wait(piece, blocks, window, send_sem, recv_sem):
@@ -263,25 +282,26 @@
     lax.fori_loop(1, 16, arrive, 0)
 
 
-def far_drain(piece, blocks, window, send_sem, recv_sem):
-    ty, tx, pos, y, zh, x = coordinates()
-
-    @pl.when(y >= 2)
-    def _():
-        far_copy(0, piece, blocks, window, send_sem, recv_sem).wait_send()
+def far_drain(piece, turned, *far):
+    ty, tx, pos, y, zh, x = coordinates()
+
+    @pl.when(turned_row(y, turned) >= 2)
+    def _():
+        far_copy(0, piece, None, turned, *far).wait_send()
 
     for j in range(1, 8):
-        far_copy(j, piece, blocks, window, send_sem, recv_sem).wait_send()
+        far_copy(j, piece, None, turned, *far).wait_send()
 
 
 def return_copy(j, piece, gradient, arrived, send_sem, recv_sem):
     ty, tx, pos, y, zh, x = coordinates()
     t = (y * 4 + x + j) % 16
+    slot = (turned_row(y, ty) % 2) * 4 + x
     return pltpu.make_async_remote_copy(
         src_ref=gradient.at[pl.ds(2 * piece, 2), pl.ds(2 * (t // 4), 2), t % 4],
-        dst_ref=arrived.at[piece, (y % 2) * 4 + x],
+        dst_ref=arrived.at[piece, slot],
         send_sem=send_sem.at[piece, j],
-        recv_sem=recv_sem.at[piece, (y % 2) * 4 + x],
+        recv_sem=recv_sem.at[piece, slot],
         device_id=peer(ty, tx, position(t // 4, zh, t % 4)),
         device_id_type=MESH,
     )
@@ -289,6 +309,7 @@
 
 def return_start(piece, gradient, arrived, send_sem, recv_sem):
     ty, tx, pos, y, zh, x = coordinates()
+    slot = (turned_row(y, ty) % 2) * 4 + x
 
     def leave(j, carry):
         return_copy(j, piece, gradient, arrived, send_sem, recv_sem).start()
@@ -296,12 +317,13 @@
 
     lax.fori_loop(1, 16, leave, 0)
     for part in range(2):
-        arrived[piece, (y % 2) * 4 + x, part] = gradient[2 * piece + part, pl.ds(2 * y, 2), x]
+        arrived[piece, slot, part] = gradient[2 * piece + part, pl.ds(2 * y, 2), x]
 
 
 def return_wait(piece, gradient, arrived, send_sem, recv_sem):
     ty, tx, pos, y, zh, x = coordinates()
-    base = (y % 2) * 4 + x
+    slot_row = turned_row(y, ty)
+    base = (slot_row % 2) * 4 + x
 
     def wait_for(s):
         pltpu.make_async_remote_copy(
@@ -309,11 +331,11 @@
             dst_ref=arrived.at[piece, s],
             send_sem=send_sem.at[piece, 0],
             recv_sem=recv_sem.at[piece, s],
-            device_id=peer(ty, tx, position(s // 4, zh, s % 4)),
+            device_id=peer(ty, tx, position(turned_row(s // 4, ty), zh, s % 4)),
             device_id_type=MESH,
         ).wait_recv()
 
-    @pl.when(y >= 2)
+    @pl.when(slot_row >= 2)
     def _():
         wait_for(base)
 
@@ -331,27 +353,29 @@
 
 def add_returned(piece, offsets, arrived, sums):
     ty, tx, pos, y, zh, x = coordinates()
-    swaps = []
-    for j in range(8):
-        target = position(j // 4, zh, j % 4)
-        swaps.append((row_swap(offsets[target, 0]), column_swap(offsets[target, 1])))
-    for part in range(2):
-        layer = 2 * piece + part
-        own = jnp.zeros((2, 8, W), f32)
-        own_side, sibling, sibling_side = own, own, own
+    for rows in range(2):
+        totals = [[jnp.zeros((8, W), f32)] * 4 for _ in range(2)]
         for j in range(8):
-            swap_rows, swap_columns = swaps[j]
-            block = arrived[piece, j, part]
-            mine = jnp.where(swap_rows, 0.0, block)
-            theirs = jnp.where(swap_rows, block, 0.0)
-            own = own + jnp.where(swap_columns, 0.0, mine)
-            own_side = own_side + jnp.where(swap_columns, mine, 0.0)
-            sibling = sibling + jnp.where(swap_columns, 0.0, theirs)
-            sibling_side = sibling_side + jnp.where(swap_columns, theirs, 0.0)
-        sums[ty, 0, layer] = own
-        sums[ty, 1, layer] = own_side
-        sums[1 - ty, 0, layer] = sibling
-        sums[1 - ty, 1, layer] = sibling_side
+            target = position(j // 4, zh, j % 4)
+            swap_rows = row_swap(offsets[0, target], rows)
+            swap_columns = column_swap(offsets[1, target])
+            for part in range(2):
+                block = arrived[piece, j, part, rows]
+                mine = jnp.where(swap_rows, 0.0, block)
+                theirs = jnp.where(swap_rows, block, 0.0)
+                own, own_side, sibling, sibling_side = totals[part]
+                totals[part] = [
+                    own + jnp.where(swap_columns, 0.0, mine),
+                    own_side + jnp.where(swap_columns, mine, 0.0),
+                    sibling + jnp.where(swap_columns, 0.0, theirs),
+                    sibling_side + jnp.where(swap_columns, theirs, 0.0),
+                ]
+        for part in range(2):
+            layer = 2 * piece + part
+            sums[ty, 0, layer, rows] = totals[part][0]
+            sums[ty, 1, layer, rows] = totals[part][1]
+            sums[1 - ty, 0, layer, rows] = totals[part][2]
+            sums[1 - ty, 1, layer, rows] = totals[part][3]
 
 
 def sum_copy(index, role, piece, sums, parts_own, parts_side, send_sem, recv_sem):
@@ -417,21 +441,53 @@
     return jnp.dot(left, right, preferred_element_type=f32)
 
 
-def transform(real_part, imag_part, right, left, inverse):
-    def stacked(r, i):
-        if inverse:
-            return jnp.concatenate([jnp.concatenate([r, -i], 1), jnp.concatenate([i, r], 1)], 0)
-        return jnp.concatenate([jnp.concatenate([r, i], 1), jnp.concatenate([i, -r], 1)], 0)
-
-    real_high, real_low = split(real_part)
-    imag_high, imag_low = split(imag_part)
-    high = stacked(real_high, imag_high)
-    low = stacked(real_low, imag_low)
-    middle = product(high, right[0]) + product(low, right[0]) + product(high, right[1])
-    high, low = split(middle)
-    which = 1 if inverse else 0
-    result = product(left[which, 0], high) + product(left[which, 0], low) + product(left[which, 1], high)
-    return result[:W], result[W:]
+def from_right(value, table):
+    high, low = split(value)
+    return product(high, table[0]) + product(low, table[0]) + product(high, table[1])
+
+
+def from_left(table, value):
+    high, low = split(value)
+    return product(table[0], high) + product(table[0], low) + product(table[1], high)
+
+
+def transform(real_part, imag_part, right, left):
+    join = jnp.concatenate
+    h = W // 2
+    a, b, c, d = real_part[:, :h], real_part[:, h:], imag_part[:, :h], imag_part[:, h:]
+    even = from_right(join([a + b, c + d], 1), right[0, 0])
+    odd = from_right(join([a - b, c - d], 1), right[0, 1])
+    real_part, imag_part = join([even[:, :h], odd[:, :h]], 1), join([even[:, h:], odd[:, h:]], 1)
+    a, b, c, d = real_part[:h], real_part[h:], imag_part[:h], imag_part[h:]
+    even = from_left(left[0, 0], join([a + b, c + d], 0))
+    odd = from_left(left[0, 1], join([a - b, c - d], 0))
+    return join([even[:h], odd[:h]], 0), join([even[h:], odd[h:]], 0)
+
+
+def inverse(real_part, imag_part, right, left):
+    join = jnp.concatenate
+    h = W // 2
+    even = from_right(join([real_part[:, :h], imag_part[:, :h]], 1), right[1, 0])
+    odd = from_right(join([real_part[:, h:], imag_part[:, h:]], 1), right[1, 1])
+    total, rest = even + odd, even - odd
+    real_part, imag_part = join([total[:, :h], rest[:, :h]], 1), join([total[:, h:], rest[:, h:]], 1)
+    even = from_left(left[1, 0], join([real_part[:h], imag_part[:h]], 0))
+    odd = from_left(left[1, 1], join([real_part[h:], imag_part[h:]], 0))
+    total, rest = even + odd, even - odd
+    return join([total[:h], rest[:h]], 0), join([total[h:], rest[h:]], 0)
+
+
+def parts_of(value, count):
+    parts = []
+    for _ in range(count):
+        parts.append(value.astype(bf16))
+        value = value - parts[-1].astype(f32)
+    return parts
+
+
+def reordered(value, first, second, count):
+    value = sum(product(first, part) for part in parts_of(value, count))
+    return sum(product(part, second) for part in parts_of(value, count))
 
 
 def complex_product(first_real, first_imag, second_real, second_imag):
@@ -441,10 +497,9 @@
     )
 
 
-def shifted_probe(offsets, illumination):
-    pos = lax.axis_index("pos")
-    down = (offsets[pos, 0] + 192) % 256
-    across = (offsets[pos, 1] + 192) % 256
+def shifted_probe(offsets, slot, illumination):
+    down = (offsets[0, slot] + 192) % 256
+    across = (offsets[1, slot] + 192) % 256
     return [pltpu.roll(pltpu.roll(illumination[part], down, 0), across, 1) for part in range(2)]
 
 
@@ -454,14 +509,14 @@
 
 def between_field(window, probe, slab, right, left):
     entering = complex_product(probe[0], probe[1], layer_of(window, 0), layer_of(window, 1))
-    spectrum = transform(entering[0], entering[1], right, left, False)
+    spectrum = transform(entering[0], entering[1], right, left)
     spectrum = complex_product(spectrum[0], spectrum[1], slab[0], slab[1])
-    return transform(spectrum[0], spectrum[1], right, left, True)
+    return inverse(spectrum[0], spectrum[1], right, left)
 
 
 def farfield_of(between, window, right, left):
     leaving = complex_product(between[0], between[1], layer_of(window, 2), layer_of(window, 3))
-    return transform(leaving[0], leaving[1], right, left, False)
+    return transform(leaving[0], leaving[1], right, left)
 
 
 def kernel(
@@ -474,6 +529,7 @@
     phase_hbm,
     right_hbm,
     left_hbm,
+    order_hbm,
     new_rows,
     new_momentum,
     amplitude,
@@ -482,6 +538,8 @@
     phase,
     right,
     left,
+    order,
+    ordered_measured,
     probe,
     slab,
     between_kept,
@@ -497,6 +555,7 @@
     parts_own,
     parts_side,
     local_sem,
+    measured_sem,
     close_send_first,
     close_recv_first,
     close_send_second,
@@ -518,13 +577,18 @@
                 (phase_hbm, phase),
                 (illumination_hbm, illumination),
                 (right_hbm, right),
+                (order_hbm, order),
                 (left_hbm, left),
                 (measured_hbm, measured),
             )
         )
     ]
 
-    @pl.when(y < 2)
+    works = (y < 2) | (ty == 1)
+    slot_row = jnp.where(y < 2, y, 3 - y)
+    slot = position(slot_row, zh, x)
+
+    @pl.when(works)
     def _():
         for load in loads:
             load.start()
@@ -541,20 +605,44 @@
     summed = (sums, parts_own, parts_side, sum_send, sum_recv)
     for piece in (0, 1):
         close_start(piece, *close_first)
-    for piece in (0, 1):
-        close_wait(piece, *close_first)
-        far_start(piece, offsets, held_first, *far_first)
-    live = jnp.where(pos < counts[0, 0], 1.0, 0.0)
-
-    @pl.when(y < 2)
+    for half in (0, 1):
+        for piece in (0, 1):
+            close_wait(piece, half, *close_first)
+            far_start(piece, half, ty, offsets, held_first, *far_first)
+    live = jnp.where(slot < counts[0, 0], 1.0, 0.0)
+    move_measured = pltpu.make_async_remote_copy(
+        src_ref=ordered_measured,
+        dst_ref=ordered_measured,
+        send_sem=measured_sem.at[0],
+        recv_sem=measured_sem.at[1],
+        device_id=peer(ty, tx, position(3 - y, zh, x)),
+        device_id_type=MESH,
+    )
+
+    @pl.when(works)
     def _():
         for load in loads:
             load.wait()
-        slab[0] = jnp.cos(phase[...])
-        slab[1] = jnp.sin(phase[...])
-        shifted = shifted_probe(offsets, illumination)
+
+    @pl.when(y < 2)
+    def _():
+        ordered_measured[...] = reordered(measured[...], order[0], order[1], 3)
+
+    @pl.when((y < 2) & (ty == 1))
+    def _():
+        move_measured.start()
+
+    @pl.when(works)
+    def _():
+        angles = reordered(phase[...], order[0], order[1], 3)
+        slab[0] = jnp.cos(angles)
+        slab[1] = jnp.sin(angles)
+        shifted = shifted_probe(offsets, slot, illumination)
         probe[0] = shifted[0]
         probe[1] = shifted[1]
+
+    @pl.when(turned_row(y, ty) < 2)
+    def _():
         far_wait(0, *far_first)
         between = between_field(window_first, probe, slab, right, left)
         between_kept[0] = between[0]
@@ -562,16 +650,21 @@
         far_wait(1, *far_first)
         farfield = farfield_of(between, window_first, right, left)
         magnitude = jnp.sqrt(farfield[0] * farfield[0] + farfield[1] * farfield[1])
-        keeping = (1.0 - measured[...] / jnp.maximum(magnitude, magnitude_floor)) * live
-        backward = transform(farfield[0] * keeping, farfield[1] * keeping, right, left, True)
+
+        @pl.when(ty == 1)
+        def _():
+            move_measured.wait_recv()
+
+        keeping = (1.0 - ordered_measured[...] / jnp.maximum(magnitude, magnitude_floor)) * live
+        backward = inverse(farfield[0] * keeping, farfield[1] * keeping, right, left)
         grad_second = complex_product(between_kept[0], -between_kept[1], backward[0], backward[1])
         gradient[2] = grad_second[0].reshape(8, 4, 8, W)
         gradient[3] = grad_second[1].reshape(8, 4, 8, W)
         return_start(1, *returned)
         toward = complex_product(layer_of(window_first, 2), -layer_of(window_first, 3), backward[0], backward[1])
-        spectrum = transform(toward[0], toward[1], right, left, False)
+        spectrum = transform(toward[0], toward[1], right, left)
         spectrum = complex_product(spectrum[0], spectrum[1], slab[0], -slab[1])
-        incoming = transform(spectrum[0], spectrum[1], right, left, True)
+        incoming = inverse(spectrum[0], spectrum[1], right, left)
         grad_first = complex_product(probe[0], -probe[1], incoming[0], incoming[1])
         gradient[0] = grad_first[0].reshape(8, 4, 8, W)
         gradient[1] = grad_first[1].reshape(8, 4, 8, W)
@@ -592,8 +685,9 @@
             new_momentum[layer] = velocity
             new_rows[layer] = rows[layer] - step_length * velocity
         close_start(piece, *close_second)
-        close_wait(piece, *close_second)
-        far_start(piece, offsets, held_second, *far_second)
+        for half in (0, 1):
+            close_wait(piece, half, *close_second)
+            far_start(piece, half, 0, offsets, held_second, *far_second)
 
     @pl.when(y < 2)
     def _():
@@ -601,7 +695,8 @@
         between = between_field(window_second, probe, slab, right, left)
         far_wait(1, *far_second)
         farfield = farfield_of(between, window_second, right, left)
-        amplitude[...] = jnp.sqrt(farfield[0] * farfield[0] + farfield[1] * farfield[1]) * live
+        magnitude = jnp.sqrt(farfield[0] * farfield[0] + farfield[1] * farfield[1]) * live
+        amplitude[...] = reordered(magnitude, order[1], order[0], 2)
 
     @pl.when(y >= 2)
     def _():
@@ -610,19 +705,23 @@
     for piece in (0, 1):
         close_drain(piece, *close_first)
         close_drain(piece, *close_second)
-        far_drain(piece, *far_first)
-        far_drain(piece, *far_second)
+        far_drain(piece, ty, *far_first)
+        far_drain(piece, 0, *far_second)
         sum_each(piece, "sent", *summed)
 
-    @pl.when(y < 2)
+    @pl.when(turned_row(y, ty) < 2)
     def _():
         for piece in (0, 1):
             return_drain(piece, *returned)
 
+    @pl.when((y < 2) & (ty == 1))
+    def _():
+        move_measured.wait_send()
+
 
 def shards(object_field, momentum, measured, illumination, slab_phase, offsets, entry_counts):
     rows = object_field.reshape(4, 8, W)
-    right, left = (jnp.asarray(t) for t in tables(W))
+    right, left, order = (jnp.asarray(t) for t in tables(W))
     dma = pltpu.SemaphoreType.DMA
     close = len(ROLES)
     window_shape = (4, 8, 4, 8, W)
@@ -639,7 +738,7 @@
             jax.ShapeDtypeStruct((4, 8, W), f32),
             jax.ShapeDtypeStruct((W, W), f32),
         ),
-        in_specs=[smem, smem, vmem, vmem, remain, remain, remain, remain, remain],
+        in_specs=[smem, smem, vmem, vmem, remain, remain, remain, remain, remain, remain],
         out_specs=[vmem, vmem, vmem],
         scratch_shapes=[
             pltpu.VMEM((W, W), f32),
@@ -647,6 +746,8 @@
             pltpu.VMEM((W, W), f32),
             pltpu.VMEM(right.shape, bf16),
             pltpu.VMEM(left.shape, bf16),
+            pltpu.VMEM(order.shape, bf16),
+            pltpu.VMEM((W, W), f32),
             pltpu.VMEM(field, f32),
             pltpu.VMEM(field, f32),
             pltpu.VMEM(field, f32),
@@ -661,7 +762,8 @@
             pltpu.VMEM(held_shape, f32),
             pltpu.VMEM((4, 4, 8, W), f32),
             pltpu.VMEM((4, 4, 8, W), f32),
-            dma((5,)),
+            dma((6,)),
+            dma((2,)),
             dma((2, close)),
             dma((2, close)),
             dma((2, close)),
@@ -680,7 +782,7 @@
         ),
         name="iterate",
     )(
-        offsets[0, 0],
+        offsets[0, 0].T,
         entry_counts,
         rows,
         momentum.reshape(4, 8, W),
@@ -689,6 +791,7 @@
         slab_phase,
         right,
         left,
+        order,
     )
     return (
         new_rows.reshape(2, 2, 8, W),

time: 91.3 us -> 71.2 us (0.78)
  Pallas kernels: 79.1 us -> 66 us
  local copies, waits for them, and re-layouts: 9.78 us -> 3.67 us
    pallas_call x1, Pallas kernels: 79.1 us -> 66 us  [shards(): pl.pallas_call(kernel, out_shape=(jax.ShapeDtypeStruct((4, 8, W), f32), j...]
    unnamed x17 -> x5, local copies, waits for them, and re-layouts: 9.02 us -> 3.67 us
where the time goes in v3:
time: 71.2 us; the launch traced here: 71 us
  Pallas kernels  66 us (93%)
  local copies, waits for them, and re-layouts  3.67 us (5%)
  between operations  1.3 us (2%)
    pallas_call x1, Pallas kernels, shards(): pl.pallas_call(kernel, out_shape=(jax.ShapeDtypeStruct((4, 8, W), f32), j...  66 us
    unnamed x5, local copies, waits for them, and re-layouts  3.67 us

profile of v3, /device:TPU:1, one launch (start us, length us, event | category | flops | bytes accessed | tf_op | source)
XLA Modules:
  0.0 71.0 jit_solution(13419367489951462590)
XLA Ops:
  1.3 66.0 %iterate.1 = (f32[4,8,256]{2,1,0:T(8,128)}, f32[4,8,256]{2,1,0:T(8,128)}, f32[256,256]{1,0:T(8,128)}) custom-call(s32[2,32]{1,0:T(2,128)} %bitcast.15, s32[1,1]{1,0:T(1,128)S(6)} %copy.16.counts, f32[4,8,256]{2,1,0:T(8,128)} %bitcast.11, f32[4,8,256]{2,1,0:T(8,128)} %bitcast.12, f32[256,256]{1,0:T(8,128)} %bitcast.10, f32[2,256,256]{2,1,0:T(8,128)} %illumination_hbm.1, ...), custom_call_target="tpu_custom_call" | custom-call | tf_op jit(solution)/shard_map/iterate/pallas_call | solution.py:734
  67.3 0.0 copy-start
  67.3 1.4 %copy.17 = f32[2,2,8,256]{3,2,1,0:T(8,128)} copy(f32[2,2,8,256]{3,2,1,0:T(8,128)} %bitcast.14) | data formatting | bytes 65536
  68.7 0.0 copy-done
  68.7 0.6 copy.18
  69.3 1.7 %copy.19 = f32[1,1,1,256,256]{4,3,2,1,0:T(8,128)} copy(f32[1,1,1,256,256]{4,3,2,1,0:T(8,128)} %bitcast.9) | data formatting | bytes 524288
Async XLA Ops:
  67.3 1.4 %copy-start = (f32[4,8,256]{2,1,0:T(8,128)S(1)}, f32[4,8,256]{2,1,0:T(8,128)}, u32[]{:S(2)}) copy-start(f32[4,8,256]{2,1,0:T(8,128)} %get-tuple-element.7) | copy-start | bytes 98308

commit v4 on v3

--- a/solution.py
+++ b/solution.py
@@ -674,6 +674,7 @@
         return_wait(piece, *returned)
         add_returned(piece, offsets, arrived, sums)
         sum_each(piece, "start", *summed)
+    for piece in (1, 0):
         sum_each(piece, "recv", *summed)
         for layer in (2 * piece, 2 * piece + 1):
             total = sums[ty, 0, layer, zh]
@@ -685,9 +686,9 @@
             new_momentum[layer] = velocity
             new_rows[layer] = rows[layer] - step_length * velocity
         close_start(piece, *close_second)
-        for half in (0, 1):
-            close_wait(piece, half, *close_second)
-            far_start(piece, half, 0, offsets, held_second, *far_second)
+    for piece, half in ((1, 0), (0, 0), (0, 1), (1, 1)):
+        close_wait(piece, half, *close_second)
+        far_start(piece, half, 0, offsets, held_second, *far_second)
 
     @pl.when(y < 2)
     def _():
@@ -717,6 +718,11 @@
     @pl.when((y < 2) & (ty == 1))
     def _():
         move_measured.wait_send()
+
+
+def hand_over(*refs):
+    for source, target in zip(refs[:3], refs[3:]):
+        target[...] = source[...]
 
 
 def shards(object_field, momentum, measured, illumination, slab_phase, offsets, entry_counts):
@@ -731,13 +737,14 @@
     vmem = pl.BlockSpec(memory_space=pltpu.VMEM)
     smem = pl.BlockSpec(memory_space=pltpu.SMEM)
     remain = pl.BlockSpec(memory_space=pl.ANY)
-    new_rows, new_momentum, amplitude = pl.pallas_call(
+    shapes = (
+        jax.ShapeDtypeStruct((4, 8, W), f32),
+        jax.ShapeDtypeStruct((4, 8, W), f32),
+        jax.ShapeDtypeStruct((W, W), f32),
+    )
+    results = pl.pallas_call(
         kernel,
-        out_shape=(
-            jax.ShapeDtypeStruct((4, 8, W), f32),
-            jax.ShapeDtypeStruct((4, 8, W), f32),
-            jax.ShapeDtypeStruct((W, W), f32),
-        ),
+        out_shape=shapes,
         in_specs=[smem, smem, vmem, vmem, remain, remain, remain, remain, remain, remain],
         out_specs=[vmem, vmem, vmem],
         scratch_shapes=[
@@ -793,6 +800,14 @@
         left,
         order,
     )
+    new_rows, new_momentum, amplitude = pl.pallas_call(
+        hand_over,
+        out_shape=shapes,
+        in_specs=[vmem] * 3,
+        out_specs=[vmem] * 3,
+        compiler_params=pltpu.CompilerParams(vmem_limit_bytes=VMEM_LIMIT),
+        name="hand_over",
+    )(*results)
     return (
         new_rows.reshape(2, 2, 8, W),
         new_momentum.reshape(2, 2, 8, W),

time: 71.2 us -> 64.7 us (0.909)
  local copies, waits for them, and re-layouts: 3.67 us -> 0 us
  Pallas kernels: 66 us -> 63.2 us
    unnamed x5 -> x0, local copies, waits for them, and re-layouts: 3.67 us -> none
    pallas_call x1 -> x2, Pallas kernels: 66 us -> 63.2 us  [the longest x1 61.5 us: shards(): pl.pallas_call(kernel, out_shape=shapes, in_specs=[smem, smem, vmem, vmem...]
where the time goes in v4:
time: 64.7 us; the launch traced here: 64.5 us
  Pallas kernels  63.2 us (98%)
  between operations  1.29 us (2%)
    pallas_call x1, Pallas kernels, shards(): pl.pallas_call(kernel, out_shape=shapes, in_specs=[smem, smem, vmem, vmem...  61.5 us
    pallas_call x1, Pallas kernels, shards(): pl.pallas_call(hand_over, out_shape=shapes, in_specs=[vmem] * 3, out_spec...  1.72 us

profile of v4, /device:TPU:1, one launch (start us, length us, event | category | flops | bytes accessed | tf_op | source)
XLA Modules:
  0.0 64.5 jit_solution(6726312374256140002)
XLA Ops:
  1.3 61.5 %iterate.1 = (f32[4,8,256]{2,1,0:T(8,128)}, f32[4,8,256]{2,1,0:T(8,128)}, f32[256,256]{1,0:T(8,128)}) custom-call(s32[2,32]{1,0:T(2,128)} %bitcast.12, s32[1,1]{1,0:T(1,128)S(6)} %copy.13.counts, f32[4,8,256]{2,1,0:T(8,128)} %bitcast.10, f32[4,8,256]{2,1,0:T(8,128)} %bitcast.11, f32[256,256]{1,0:T(8,128)} %bitcast.9, f32[2,256,256]{2,1,0:T(8,128)} %illumination_hbm.1, ...), custom_call_target="tpu_custom_call" | custom-call | tf_op jit(solution)/shard_map/iterate/pallas_call | solution.py:745
  62.8 1.7 %hand_over.1 = (f32[4,8,256]{2,1,0:T(8,128)}, f32[4,8,256]{2,1,0:T(8,128)}, f32[256,256]{1,0:T(8,128)}) custom-call(f32[4,8,256]{2,1,0:T(8,128)} %get-tuple-element.9.refs_0_, f32[4,8,256]{2,1,0:T(8,128)} %get-tuple-element.10.refs_1_, f32[256,256]{1,0:T(8,128)} %get-tuple-element.11.refs_2_), custom_call_target="tpu_custom_call" | custom-call | tf_op jit(solution)/shard_map/hand_over/pallas_call | solution.py:803

commit v5 on v4

--- a/solution.py
+++ b/solution.py
@@ -85,7 +85,7 @@
         pl.when(condition)(body)
 
 
-def enter():
+def enter(clear):
     ty, tx, pos, y, zh, x = coordinates()
     barrier = pltpu.get_barrier_semaphore()
     outer = (y == 0) | (y == 3)
@@ -110,15 +110,18 @@
 
         lax.fori_loop(0, count, body, 0)
 
-    @pl.when((y < 2) | (ty == 1))
+    everyone = (y < 2) | (ty == 1)
+
+    @pl.when(everyone)
     def _():
         greet(me + 1, 15, 16)
-        pl.semaphore_wait(barrier, near + 15)
-
-    @pl.when((y >= 2) & (ty == 0))
+
+    @pl.when(jnp.logical_not(everyone))
     def _():
         greet(small, 8, 8)
-        pl.semaphore_wait(barrier, near + 8)
+
+    clear()
+    pl.semaphore_wait(barrier, near + jnp.where(everyone, 15, 8))
 
 
 def turned_row(y, turned):
@@ -293,44 +296,64 @@
         far_copy(j, piece, None, turned, *far).wait_send()
 
 
-def return_copy(j, piece, gradient, arrived, send_sem, recv_sem):
+def chosen_rows(half):
+    zh = coordinates()[4]
+    return 1 - zh if half else zh
+
+
+def return_copy(j, piece, half, gradient, arrived, send_sem, recv_sem):
     ty, tx, pos, y, zh, x = coordinates()
     t = (y * 4 + x + j) % 16
     slot = (turned_row(y, ty) % 2) * 4 + x
+    layers = pl.ds(2 * piece, 2)
+    if half is None:
+        source, target = gradient.at[layers, pl.ds(2 * (t // 4), 2), t % 4], arrived.at[piece, slot]
+    else:
+        rows = chosen_rows(half)
+        source, target = gradient.at[layers, 2 * (t // 4) + rows, t % 4], arrived.at[piece, slot, :, rows]
     return pltpu.make_async_remote_copy(
-        src_ref=gradient.at[pl.ds(2 * piece, 2), pl.ds(2 * (t // 4), 2), t % 4],
-        dst_ref=arrived.at[piece, slot],
+        src_ref=source,
+        dst_ref=target,
         send_sem=send_sem.at[piece, j],
-        recv_sem=recv_sem.at[piece, slot],
+        recv_sem=recv_sem.at[piece, half or 0, slot],
         device_id=peer(ty, tx, position(t // 4, zh, t % 4)),
         device_id_type=MESH,
     )
 
 
-def return_start(piece, gradient, arrived, send_sem, recv_sem):
+def return_start(piece, half, gradient, arrived, send_sem, recv_sem):
     ty, tx, pos, y, zh, x = coordinates()
     slot = (turned_row(y, ty) % 2) * 4 + x
 
     def leave(j, carry):
-        return_copy(j, piece, gradient, arrived, send_sem, recv_sem).start()
+        return_copy(j, piece, half, gradient, arrived, send_sem, recv_sem).start()
         return carry
 
     lax.fori_loop(1, 16, leave, 0)
     for part in range(2):
-        arrived[piece, slot, part] = gradient[2 * piece + part, pl.ds(2 * y, 2), x]
-
-
-def return_wait(piece, gradient, arrived, send_sem, recv_sem):
+        if half is None:
+            arrived[piece, slot, part] = gradient[2 * piece + part, pl.ds(2 * y, 2), x]
+        else:
+            rows = chosen_rows(half)
+            arrived[piece, slot, part, rows] = gradient[2 * piece + part, 2 * y + rows, x]
+
+
+def return_wait(piece, half, gradient, arrived, send_sem, recv_sem):
     ty, tx, pos, y, zh, x = coordinates()
     slot_row = turned_row(y, ty)
     base = (slot_row % 2) * 4 + x
+    layers = pl.ds(2 * piece, 2)
 
     def wait_for(s):
+        if half is None:
+            source, target = gradient.at[layers, pl.ds(0, 2), 0], arrived.at[piece, s]
+        else:
+            source, target = gradient.at[layers, 0, 0], arrived.at[piece, s, :, chosen_rows(half)]
         pltpu.make_async_remote_copy(
-            src_ref=gradient.at[pl.ds(2 * piece, 2), pl.ds(0, 2), 0],
-            dst_ref=arrived.at[piece, s],
+            src_ref=source,
+            dst_ref=target,
             send_sem=send_sem.at[piece, 0],
-            recv_sem=recv_sem.at[piece, s],
+            recv_sem=recv_sem.at[piece, half or 0, s],
             device_id=peer(ty, tx, position(turned_row(s // 4, ty), zh, s % 4)),
             device_id_type=MESH,
         ).wait_recv()
@@ -345,37 +368,37 @@
 
 def return_drain(piece, gradient, arrived, send_sem, recv_sem):
     def left(j, carry):
-        return_copy(j, piece, gradient, arrived, send_sem, recv_sem).wait_send()
+        return_copy(j, piece, None, gradient, arrived, send_sem, recv_sem).wait_send()
         return carry
 
     lax.fori_loop(1, 16, left, 0)
 
 
-def add_returned(piece, offsets, arrived, sums):
-    ty, tx, pos, y, zh, x = coordinates()
-    for rows in range(2):
-        totals = [[jnp.zeros((8, W), f32)] * 4 for _ in range(2)]
-        for j in range(8):
-            target = position(j // 4, zh, j % 4)
-            swap_rows = row_swap(offsets[0, target], rows)
-            swap_columns = column_swap(offsets[1, target])
-            for part in range(2):
-                block = arrived[piece, j, part, rows]
-                mine = jnp.where(swap_rows, 0.0, block)
-                theirs = jnp.where(swap_rows, block, 0.0)
-                own, own_side, sibling, sibling_side = totals[part]
-                totals[part] = [
-                    own + jnp.where(swap_columns, 0.0, mine),
-                    own_side + jnp.where(swap_columns, mine, 0.0),
-                    sibling + jnp.where(swap_columns, 0.0, theirs),
-                    sibling_side + jnp.where(swap_columns, theirs, 0.0),
-                ]
+def add_returned(piece, half, offsets, arrived, sums):
+    ty, tx, pos, y, zh, x = coordinates()
+    rows = chosen_rows(half)
+    totals = [[jnp.zeros((8, W), f32)] * 4 for _ in range(2)]
+    for j in range(8):
+        target = position(j // 4, zh, j % 4)
+        swap_rows = row_swap(offsets[0, target], rows)
+        swap_columns = column_swap(offsets[1, target])
         for part in range(2):
-            layer = 2 * piece + part
-            sums[ty, 0, layer, rows] = totals[part][0]
-            sums[ty, 1, layer, rows] = totals[part][1]
-            sums[1 - ty, 0, layer, rows] = totals[part][2]
-            sums[1 - ty, 1, layer, rows] = totals[part][3]
+            block = arrived[piece, j, part, rows]
+            mine = jnp.where(swap_rows, 0.0, block)
+            theirs = jnp.where(swap_rows, block, 0.0)
+            own, own_side, sibling, sibling_side = totals[part]
+            totals[part] = [
+                own + jnp.where(swap_columns, 0.0, mine),
+                own_side + jnp.where(swap_columns, mine, 0.0),
+                sibling + jnp.where(swap_columns, 0.0, theirs),
+                sibling_side + jnp.where(swap_columns, theirs, 0.0),
+            ]
+    for part in range(2):
+        layer = 2 * piece + part
+        sums[ty, 0, layer, rows] = totals[part][0]
+        sums[ty, 1, layer, rows] = totals[part][1]
+        sums[1 - ty, 0, layer, rows] = totals[part][2]
+        sums[1 - ty, 1, layer, rows] = totals[part][3]
 
 
 def sum_copy(index, role, piece, sums, parts_own, parts_side, send_sem, recv_sem):
@@ -398,10 +421,12 @@
     )
 
 
-def sum_each(piece, action, *refs):
+def sum_each(piece, action, half, *refs):
     ty, tx, pos, y, zh, x = coordinates()
     takes, gives = sibling_facts()
     for index, role in enumerate(ROLES):
+        if half not in (None, role[1]):
+            continue
         copy = sum_copy(index, role, piece, *refs)
         if action == "recv":
             when(has_role(role, gives, tx > 0, tx < 3), copy.wait_recv)
@@ -520,10 +545,10 @@
 
 
 def kernel(
-    offsets,
-    counts,
-    rows,
-    momentum,
+    offsets_hbm,
+    counts_hbm,
+    rows_hbm,
+    momentum_hbm,
     measured_hbm,
     illumination_hbm,
     phase_hbm,
@@ -533,6 +558,10 @@
     new_rows,
     new_momentum,
     amplitude,
+    offsets,
+    counts,
+    rows,
+    momentum,
     measured,
     illumination,
     phase,
@@ -580,23 +609,36 @@
                 (order_hbm, order),
                 (left_hbm, left),
                 (measured_hbm, measured),
+                (counts_hbm, counts),
+                (rows_hbm, rows),
+                (offsets_hbm, offsets),
+                (momentum_hbm, momentum),
             )
         )
     ]
+    loads, (counts_load, rows_load, offsets_load, momentum_load) = loads[:-4], loads[-4:]
 
     works = (y < 2) | (ty == 1)
     slot_row = jnp.where(y < 2, y, 3 - y)
     slot = position(slot_row, zh, x)
 
-    @pl.when(works)
-    def _():
-        for load in loads:
-            load.start()
-
-    clear_missing(held_first)
-    clear_missing(held_second)
-    clear_parts(parts_own, parts_side)
-    enter()
+    def begin():
+        rows_load.start()
+        offsets_load.start()
+        counts_load.start()
+        momentum_load.start()
+
+        @pl.when(works)
+        def _():
+            for load in loads:
+                load.start()
+
+        clear_missing(held_first)
+        clear_missing(held_second)
+        clear_parts(parts_own, parts_side)
+        rows_load.wait()
+
+    enter(begin)
     close_first = (rows, held_first, close_send_first, close_recv_first)
     close_second = (new_rows, held_second, close_send_second, close_recv_second)
     far_first = (blocks_first, window_first, far_send_first, far_recv_first)
@@ -605,6 +647,8 @@
     summed = (sums, parts_own, parts_side, sum_send, sum_recv)
     for piece in (0, 1):
         close_start(piece, *close_first)
+    offsets_load.wait()
+    counts_load.wait()
     for half in (0, 1):
         for piece in (0, 1):
             close_wait(piece, half, *close_first)
@@ -660,7 +704,7 @@
         grad_second = complex_product(between_kept[0], -between_kept[1], backward[0], backward[1])
         gradient[2] = grad_second[0].reshape(8, 4, 8, W)
         gradient[3] = grad_second[1].reshape(8, 4, 8, W)
-        return_start(1, *returned)
+        return_start(1, None, *returned)
         toward = complex_product(layer_of(window_first, 2), -layer_of(window_first, 3), backward[0], backward[1])
         spectrum = transform(toward[0], toward[1], right, left)
         spectrum = complex_product(spectrum[0], spectrum[1], slab[0], -slab[1])
@@ -668,14 +712,20 @@
         grad_first = complex_product(probe[0], -probe[1], incoming[0], incoming[1])
         gradient[0] = grad_first[0].reshape(8, 4, 8, W)
         gradient[1] = grad_first[1].reshape(8, 4, 8, W)
-        return_start(0, *returned)
-
+        for half in (1, 0):
+            return_start(0, half, *returned)
+
+    return_wait(1, None, *returned)
+    for half in (1, 0):
+        add_returned(1, half, offsets, arrived, sums)
+        sum_each(1, "start", half, *summed)
+    for half in (1, 0):
+        return_wait(0, half, *returned)
+        add_returned(0, half, offsets, arrived, sums)
+        sum_each(0, "start", half, *summed)
+    momentum_load.wait()
     for piece in (1, 0):
-        return_wait(piece, *returned)
-        add_returned(piece, offsets, arrived, sums)
-        sum_each(piece, "start", *summed)
-    for piece in (1, 0):
-        sum_each(piece, "recv", *summed)
+        sum_each(piece, "recv", None, *summed)
         for layer in (2 * piece, 2 * piece + 1):
             total = sums[ty, 0, layer, zh]
             for part in range(4):
@@ -708,7 +758,7 @@
         close_drain(piece, *close_second)
         far_drain(piece, ty, *far_first)
         far_drain(piece, 0, *far_second)
-        sum_each(piece, "sent", *summed)
+        sum_each(piece, "sent", None, *summed)
 
     @pl.when(turned_row(y, ty) < 2)
     def _():
@@ -735,7 +785,6 @@
     blocks_shape = (2, 8, 2, 2, 8, W)
     field = (2, W, W)
     vmem = pl.BlockSpec(memory_space=pltpu.VMEM)
-    smem = pl.BlockSpec(memory_space=pltpu.SMEM)
     remain = pl.BlockSpec(memory_space=pl.ANY)
     shapes = (
         jax.ShapeDtypeStruct((4, 8, W), f32),
@@ -745,9 +794,13 @@
     results = pl.pallas_call(
         kernel,
         out_shape=shapes,
-        in_specs=[smem, smem, vmem, vmem, remain, remain, remain, remain, remain, remain],
+        in_specs=[remain] * 10,
         out_specs=[vmem, vmem, vmem],
         scratch_shapes=[
+            pltpu.SMEM((2, offsets.shape[2]), jnp.int32),
+            pltpu.SMEM((1, 1), jnp.int32),
+            pltpu.VMEM((4, 8, W), f32),
+            pltpu.VMEM((4, 8, W), f32),
             pltpu.VMEM((W, W), f32),
             pltpu.VMEM(field, f32),
             pltpu.VMEM((W, W), f32),
@@ -769,7 +822,7 @@
             pltpu.VMEM(held_shape, f32),
             pltpu.VMEM((4, 4, 8, W), f32),
             pltpu.VMEM((4, 4, 8, W), f32),
-            dma((6,)),
+            dma((10,)),
             dma((2,)),
             dma((2, close)),
             dma((2, close)),
@@ -780,7 +833,7 @@
             dma((2, 8)),
             dma((2, 16)),
             dma((2, 16)),
-            dma((2, 8)),
+            dma((2, 2, 8)),
             dma((2, close)),
             dma((2, close)),
         ],

time: 64.7 us -> 63.1 us (0.975)
  Pallas kernels: 63.2 us -> 61.6 us
    pallas_call x1, Pallas kernels: 61.5 us -> 59.9 us  [shards(): pl.pallas_call(kernel, out_shape=shapes, in_specs=[remain] * 10, out_spec...]
where the time goes in v5:
time: 63.1 us; the launch traced here: 62.9 us
  Pallas kernels  61.6 us (98%)
  between operations  1.29 us (2%)
    pallas_call x1, Pallas kernels, shards(): pl.pallas_call(kernel, out_shape=shapes, in_specs=[remain] * 10, out_spec...  59.9 us
    pallas_call x1, Pallas kernels, shards(): pl.pallas_call(hand_over, out_shape=shapes, in_specs=[vmem] * 3, out_spec...  1.72 us

profile of v5, /device:TPU:1, one launch (start us, length us, event | category | flops | bytes accessed | tf_op | source)
XLA Modules:
  0.0 62.9 jit_solution(3312976969631041484)
XLA Ops:
  1.3 59.9 %iterate.1 = (f32[4,8,256]{2,1,0:T(8,128)}, f32[4,8,256]{2,1,0:T(8,128)}, f32[256,256]{1,0:T(8,128)}) custom-call(s32[2,32]{1,0:T(2,128)} %bitcast.12, s32[1,1]{1,0:T(1,128)S(6)} %copy.13.counts_hbm, f32[4,8,256]{2,1,0:T(8,128)} %bitcast.10, f32[4,8,256]{2,1,0:T(8,128)} %bitcast.11, f32[256,256]{1,0:T(8,128)} %bitcast.9, f32[2,256,256]{2,1,0:T(8,128)} %illumination_hbm.1, ...), custom_call_target="tpu_custom_call" | custom-call | tf_op jit(solution)/shard_map/iterate/pallas_call | solution.py:794
  61.2 1.7 %hand_over.1 = (f32[4,8,256]{2,1,0:T(8,128)}, f32[4,8,256]{2,1,0:T(8,128)}, f32[256,256]{1,0:T(8,128)}) custom-call(f32[4,8,256]{2,1,0:T(8,128)} %get-tuple-element.9.refs_0_, f32[4,8,256]{2,1,0:T(8,128)} %get-tuple-element.10.refs_1_, f32[256,256]{1,0:T(8,128)} %get-tuple-element.11.refs_2_), custom_call_target="tpu_custom_call" | custom-call | tf_op jit(solution)/shard_map/hand_over/pallas_call | solution.py:856

commit v6 on v5

--- a/solution.py
+++ b/solution.py
@@ -555,9 +555,11 @@
     right_hbm,
     left_hbm,
     order_hbm,
+    new_rows_out,
+    new_momentum_out,
+    amplitude,
     new_rows,
     new_momentum,
-    amplitude,
     offsets,
     counts,
     rows,
@@ -585,6 +587,7 @@
     parts_side,
     local_sem,
     measured_sem,
+    store_sem,
     close_send_first,
     close_recv_first,
     close_send_second,
@@ -649,8 +652,8 @@
         close_start(piece, *close_first)
     offsets_load.wait()
     counts_load.wait()
-    for half in (0, 1):
-        for piece in (0, 1):
+    for piece in (0, 1):
+        for half in (0, 1):
             close_wait(piece, half, *close_first)
             far_start(piece, half, ty, offsets, held_first, *far_first)
     live = jnp.where(slot < counts[0, 0], 1.0, 0.0)
@@ -704,7 +707,8 @@
         grad_second = complex_product(between_kept[0], -between_kept[1], backward[0], backward[1])
         gradient[2] = grad_second[0].reshape(8, 4, 8, W)
         gradient[3] = grad_second[1].reshape(8, 4, 8, W)
-        return_start(1, None, *returned)
+        for half in (1, 0):
+            return_start(1, half, *returned)
         toward = complex_product(layer_of(window_first, 2), -layer_of(window_first, 3), backward[0], backward[1])
         spectrum = transform(toward[0], toward[1], right, left)
         spectrum = complex_product(spectrum[0], spectrum[1], slab[0], -slab[1])
@@ -715,8 +719,8 @@
         for half in (1, 0):
             return_start(0, half, *returned)
 
-    return_wait(1, None, *returned)
     for half in (1, 0):
+        return_wait(1, half, *returned)
         add_returned(1, half, offsets, arrived, sums)
         sum_each(1, "start", half, *summed)
     for half in (1, 0):
@@ -736,6 +740,12 @@
             new_momentum[layer] = velocity
             new_rows[layer] = rows[layer] - step_length * velocity
         close_start(piece, *close_second)
+    stores = [
+        pltpu.make_async_copy(new_rows, new_rows_out, store_sem.at[0]),
+        pltpu.make_async_copy(new_momentum, new_momentum_out, store_sem.at[1]),
+    ]
+    for store in stores:
+        store.start()
     for piece, half in ((1, 0), (0, 0), (0, 1), (1, 1)):
         close_wait(piece, half, *close_second)
         far_start(piece, half, 0, offsets, held_second, *far_second)
@@ -753,6 +763,8 @@
     def _():
         amplitude[...] = jnp.zeros_like(amplitude)
 
+    for store in stores:
+        store.wait()
     for piece in (0, 1):
         close_drain(piece, *close_first)
         close_drain(piece, *close_second)
@@ -795,8 +807,10 @@
         kernel,
         out_shape=shapes,
         in_specs=[remain] * 10,
-        out_specs=[vmem, vmem, vmem],
+        out_specs=[remain, remain, vmem],
         scratch_shapes=[
+            pltpu.VMEM((4, 8, W), f32),
+            pltpu.VMEM((4, 8, W), f32),
             pltpu.SMEM((2, offsets.shape[2]), jnp.int32),
             pltpu.SMEM((1, 1), jnp.int32),
             pltpu.VMEM((4, 8, W), f32),
@@ -823,6 +837,7 @@
             pltpu.VMEM((4, 4, 8, W), f32),
             pltpu.VMEM((4, 4, 8, W), f32),
             dma((10,)),
+            dma((2,)),
             dma((2,)),
             dma((2, close)),
             dma((2, close)),

time: 63.1 us -> 62.5 us (level)
  no operation moved by 1% of the time
where the time goes in v6:
time: 62.5 us; the launch traced here: 62.4 us
  Pallas kernels  61.1 us (98%)
  between operations  1.29 us (2%)
    pallas_call x1, Pallas kernels, shards(): pl.pallas_call(kernel, out_shape=shapes, in_specs=[remain] * 10, out_spec...  59.4 us
    pallas_call x1, Pallas kernels, shards(): pl.pallas_call(hand_over, out_shape=shapes, in_specs=[vmem] * 3, out_spec...  1.72 us

profile of v6, /device:TPU:1, one launch (start us, length us, event | category | flops | bytes accessed | tf_op | source)
XLA Modules:
  0.0 62.4 jit_solution(11712503918510272994)
XLA Ops:
  1.3 59.4 %iterate.1 = (f32[4,8,256]{2,1,0:T(8,128)}, f32[4,8,256]{2,1,0:T(8,128)}, f32[256,256]{1,0:T(8,128)}) custom-call(s32[2,32]{1,0:T(2,128)} %bitcast.12, s32[1,1]{1,0:T(1,128)S(6)} %copy.13.counts_hbm, f32[4,8,256]{2,1,0:T(8,128)} %bitcast.10, f32[4,8,256]{2,1,0:T(8,128)} %bitcast.11, f32[256,256]{1,0:T(8,128)} %bitcast.9, f32[2,256,256]{2,1,0:T(8,128)} %illumination_hbm.1, ...), custom_call_target="tpu_custom_call" | custom-call | tf_op jit(solution)/shard_map/iterate/pallas_call | solution.py:806
  60.6 1.7 %hand_over.1 = (f32[4,8,256]{2,1,0:T(8,128)}, f32[4,8,256]{2,1,0:T(8,128)}, f32[256,256]{1,0:T(8,128)}) custom-call(f32[4,8,256]{2,1,0:T(8,128)} %get-tuple-element.9.refs_0_, f32[4,8,256]{2,1,0:T(8,128)} %get-tuple-element.10.refs_1_, f32[256,256]{1,0:T(8,128)} %get-tuple-element.11.refs_2_), custom_call_target="tpu_custom_call" | custom-call | tf_op jit(solution)/shard_map/hand_over/pallas_call | solution.py:871

commit v7 on v6

--- a/solution.py
+++ b/solution.py
@@ -750,6 +750,23 @@
         close_wait(piece, half, *close_second)
         far_start(piece, half, 0, offsets, held_second, *far_second)
 
+    for store in stores:
+        store.wait()
+    for piece in (0, 1):
+        close_drain(piece, *close_first)
+        close_drain(piece, *close_second)
+        far_drain(piece, ty, *far_first)
+        sum_each(piece, "sent", None, *summed)
+
+    @pl.when(turned_row(y, ty) < 2)
+    def _():
+        for piece in (0, 1):
+            return_drain(piece, *returned)
+
+    @pl.when((y < 2) & (ty == 1))
+    def _():
+        move_measured.wait_send()
+
     @pl.when(y < 2)
     def _():
         far_wait(0, *far_second)
@@ -763,23 +780,8 @@
     def _():
         amplitude[...] = jnp.zeros_like(amplitude)
 
-    for store in stores:
-        store.wait()
     for piece in (0, 1):
-        close_drain(piece, *close_first)
-        close_drain(piece, *close_second)
-        far_drain(piece, ty, *far_first)
         far_drain(piece, 0, *far_second)
-        sum_each(piece, "sent", None, *summed)
-
-    @pl.when(turned_row(y, ty) < 2)
-    def _():
-        for piece in (0, 1):
-            return_drain(piece, *returned)
-
-    @pl.when((y < 2) & (ty == 1))
-    def _():
-        move_measured.wait_send()
 
 
 def hand_over(*refs):

time: 62.5 us -> 62.4 us (level)
  no operation moved by 1% of the time
where the time goes in v7:
time: 62.4 us; the launch traced here: 62.2 us
  Pallas kernels  61 us (98%)
  between operations  1.29 us (2%)
    pallas_call x1, Pallas kernels, shards(): pl.pallas_call(kernel, out_shape=shapes, in_specs=[remain] * 10, out_spec...  59.2 us
    pallas_call x1, Pallas kernels, shards(): pl.pallas_call(hand_over, out_shape=shapes, in_specs=[vmem] * 3, out_spec...  1.72 us

profile of v7, /device:TPU:1, one launch (start us, length us, event | category | flops | bytes accessed | tf_op | source)
XLA Modules:
  0.0 62.2 jit_solution(13002367184043645970)
XLA Ops:
  1.3 59.2 %iterate.1 = (f32[4,8,256]{2,1,0:T(8,128)}, f32[4,8,256]{2,1,0:T(8,128)}, f32[256,256]{1,0:T(8,128)}) custom-call(s32[2,32]{1,0:T(2,128)} %bitcast.12, s32[1,1]{1,0:T(1,128)S(6)} %copy.13.counts_hbm, f32[4,8,256]{2,1,0:T(8,128)} %bitcast.10, f32[4,8,256]{2,1,0:T(8,128)} %bitcast.11, f32[256,256]{1,0:T(8,128)} %bitcast.9, f32[2,256,256]{2,1,0:T(8,128)} %illumination_hbm.1, ...), custom_call_target="tpu_custom_call" | custom-call | tf_op jit(solution)/shard_map/iterate/pallas_call | solution.py:808
  60.5 1.7 %hand_over.1 = (f32[4,8,256]{2,1,0:T(8,128)}, f32[4,8,256]{2,1,0:T(8,128)}, f32[256,256]{1,0:T(8,128)}) custom-call(f32[4,8,256]{2,1,0:T(8,128)} %get-tuple-element.9.refs_0_, f32[4,8,256]{2,1,0:T(8,128)} %get-tuple-element.10.refs_1_, f32[256,256]{1,0:T(8,128)} %get-tuple-element.11.refs_2_), custom_call_target="tpu_custom_call" | custom-call | tf_op jit(solution)/shard_map/hand_over/pallas_call | solution.py:873
